TPU v7x, 512 devices: a whole 4x8x8 slice. The times are simulated.
512 devices in a mesh: grp: 16 (over x, z_lo), dev: 32 (over y, z_hi, core).
Axes of the slice: x: 4, y: 8, z: 8 (z_hi: 2, z_lo: 4; z = z_hi * 4 + z_lo), core: 2. Of those that a mesh axis runs over, the one named last changes fastest.
Arguments:
- volume: bfloat16 [64, 128, 256], P('grp', 'dev'), may hold values from -6 to 6
- w_first: bfloat16 [3, 3, 3, 32, 32], replicated, may hold values from -0.21875 to 0.21875
- w_second: bfloat16 [3, 3, 3, 32, 32], replicated, may hold values from -0.21875 to 0.21875
- w_lift: bfloat16 [256, 512], replicated, may hold values from -0.375 to 0.375
- w_coarse: bfloat16 [3, 3, 3, 512, 512], P(None, None, None, 'dev'), may hold values from -0.0546875 to 0.0546875
- w_up: bfloat16 [512, 512], replicated, may hold values from -0.25 to 0.25
Outputs:
- mixed: bfloat16 [64, 128, 256], P('grp', 'dev')
All inputs are finite; a program needn't handle non-finite values.
Results may differ from a plain program's by a relative error of at most 0.0061.
Values may be sent and summed in bfloat16 or wider, within the bound.
A program may use at most 64 MiB of HBM per device.

v0:
```python
import jax
import jax.numpy as jnp
from jax import lax
from jax.sharding import PartitionSpec as P


def with_halo(block, sides, width):
    for axis, dim in sides:
        count = lax.axis_size(axis)
        forward = [(i, i + 1) for i in range(count - 1)]
        backward = [(target, source) for source, target in forward]
        low = lax.ppermute(
            lax.slice_in_dim(block, block.shape[dim] - width, None, axis=dim), axis, forward
        )
        high = lax.ppermute(lax.slice_in_dim(block, 0, width, axis=dim), axis, backward)
        block = jnp.concatenate([low, block, high], axis=dim)
    return block


def in_blocks(x, dim, count):
    dims = x.shape
    pieces = x.reshape(*dims[:dim], count, dims[dim] // count, *dims[dim + 1 :])
    return jnp.moveaxis(pieces, dim, 0)


def sum_at_owner(x, axis, dim):
    count = lax.axis_size(axis)
    pieces = lax.all_to_all(in_blocks(x, dim, count), axis, 0, 0, tiled=True)
    return jnp.sum(pieces.astype(jnp.float32), axis=0)


def tap_offsets():
    return [
        (along_x, along_y, along_z)
        for along_x in range(3)
        for along_y in range(3)
        for along_z in range(3)
    ]


def fine_conv(slab_in, weight):
    extent_x, extent_y, packed = slab_in.shape
    channels = weight.shape[-1]
    layers = packed // channels
    padded = with_halo(slab_in, (("grp", 0), ("dev", 1)), 1)
    padded = padded.reshape(extent_x + 2, extent_y + 2, layers, channels)
    padded = jnp.pad(padded, ((0, 0), (0, 0), (1, 1), (0, 0)))
    columns = jnp.concatenate(
        [
            padded[
                along_x : along_x + extent_x,
                along_y : along_y + extent_y,
                along_z : along_z + layers,
                :,
            ]
            for along_x, along_y, along_z in tap_offsets()
        ],
        axis=-1,
    )
    preact = jnp.dot(
        columns.reshape(-1, 27 * channels),
        weight.reshape(27 * channels, channels),
        preferred_element_type=jnp.float32,
    )
    return (
        jax.nn.gelu(preact, approximate=False)
        .astype(jnp.bfloat16)
        .reshape(extent_x, extent_y, packed)
    )


def expand_half(upper, half, extent_x, extent_y, packed):
    grid = upper[:, :, :, half]
    grid = grid.transpose(0, 3, 1, 4, 2, 5, 6)
    return grid.reshape(extent_x, extent_y, packed)


def on_device(volume, w_first, w_second, w_lift, w_coarse, w_up):
    extent_x, extent_y, packed = volume.shape
    channels = w_first.shape[-1]
    layers = packed // channels
    width = w_up.shape[0]
    first_act = fine_conv(volume, w_first)
    skip_act = fine_conv(first_act, w_second)
    coarse_x, coarse_y, coarse_z = (extent_x // 2, extent_y // 2, layers // 2)
    own_rows = coarse_x * coarse_y * coarse_z
    grid = skip_act.reshape(coarse_x, 2, coarse_y, 2, coarse_z, 2, channels)
    stacked = grid.transpose(0, 2, 4, 1, 3, 5, 6).reshape(own_rows, 8 * channels)
    lifted = jax.nn.gelu(
        jnp.dot(stacked, w_lift, preferred_element_type=jnp.float32), approximate=False
    ).astype(jnp.bfloat16)
    devices = lax.axis_size("dev")
    spread = (
        lifted.reshape(coarse_x, coarse_y, coarse_z, width)
        .transpose(3, 0, 1, 2)
        .reshape(width, coarse_x, coarse_y * coarse_z)
    )
    moved = lax.all_to_all(spread, "dev", split_axis=0, concat_axis=2, tiled=True)
    in_block = moved.shape[0]
    rimmed = with_halo(moved, (("grp", 1),), 1)
    rimmed = rimmed.reshape(in_block, coarse_x + 2, devices * coarse_y, coarse_z)
    rimmed = jnp.pad(rimmed, ((0, 0), (0, 0), (1, 1), (1, 1)))
    span_y = devices * coarse_y
    columns = jnp.stack(
        [
            rimmed[
                :,
                along_x : along_x + coarse_x,
                along_y : along_y + span_y,
                along_z : along_z + coarse_z,
            ]
            for along_x, along_y, along_z in tap_offsets()
        ],
        axis=0,
    )
    columns = columns.reshape(27 * in_block, coarse_x, devices, coarse_y, coarse_z).transpose(
        0, 2, 1, 3, 4
    )
    columns = columns.reshape(27 * in_block, devices * own_rows)
    weight_rows = w_coarse.reshape(27 * in_block, width)
    summed = sum_at_owner(
        lax.dot_general(
            columns, weight_rows, (((0,), (0,)), ((), ())), preferred_element_type=jnp.float32
        ).astype(jnp.bfloat16),
        "dev",
        0,
    )
    coarse = jax.nn.gelu(summed, approximate=False).astype(jnp.bfloat16)
    upper = jnp.dot(coarse, w_up, preferred_element_type=jnp.float32)
    upper = upper.reshape(coarse_x, coarse_y, coarse_z, 2, 2, 2, 2, channels)
    gate = expand_half(upper, 0, extent_x, extent_y, packed)
    value = expand_half(upper, 1, extent_x, extent_y, packed)
    mixed = skip_act.astype(jnp.float32) * jax.nn.sigmoid(gate) + value
    return mixed.astype(jnp.bfloat16)


def solution(mesh):
    return jax.shard_map(
        on_device,
        mesh=mesh,
        in_specs=(P("grp", "dev", None), P(), P(), P(), P(None, None, None, "dev", None), P()),
        out_specs=P("grp", "dev", None),
        check_vma=False,
    )
```

profile of v0, /device:TPU:1, one launch (start us, length us, event | category | flops | bytes accessed | tf_op | source)
XLA Modules:
  0.0 130.4 jit_solution(16442635516077594034)
XLA Ops:
  0.0 0.8 fusion.146
  0.8 4.8 %collective-permute-start = (bf16[1,4,256]{2,1,0:T(4,128)(2,1)S(1)}, bf16[1,4,256]{2,1,0:T(4,128)(2,1)S(1)}, u32[]{:S(2)}, u32[]{:S(2)}) collective-permute-start(bf16[1,4,256]{2,1,0:T(4,128)(2,1)S(1)} %get-tuple-element.70), channel_id=1, source_target_pairs={{0,32},{32,64},{64,96},{96,128},{128,160},{160,192},{192,224},{224... | collective-permute-start | bytes 6152 | tf_op jit(solution)/shard_map/ppermute | solution.py:12
  5.6 1.3 collective-permute-start.1
  6.9 0.7 constant_dynamic-update-slice_fusion.1
  7.7 2.9 %collective-permute-done.1 = bf16[1,4,256]{2,1,0:T(4,128)(2,1)S(1)} collective-permute-done((bf16[1,4,256]{2,1,0:T(4,128)(2,1)S(1)}, bf16[1,4,256]{2,1,0:T(4,128)(2,1)S(1)}, u32[]{:S(2)}, u32[]{:S(2)}) %collective-permute-start.1) | collective-permute-done | bytes 2080 | tf_op jit(solution)/shard_map/ppermute | solution.py:15
  10.6 11.1 %collective-permute-start.2 = (bf16[6,1,256]{2,1,0:T(2,128)(2,1)S(1)}, bf16[6,1,256]{2,1,0:T(2,128)(2,1)S(1)}, u32[]{:S(2)}, u32[]{:S(2)}) collective-permute-start(bf16[6,1,256]{2,1,0:T(2,128)(2,1)S(1)} %get-tuple-element.65), channel_id=1, source_target_pairs={{0,1},{1,2},{2,3},{3,4},{4,5},{5,6},{6,7},{7,8},{8,9},{9,10},{10,1... | collective-permute-start | bytes 9224 | tf_op jit(solution)/shard_map/ppermute | solution.py:12
  21.7 1.9 %collective-permute-start.3 = (bf16[6,1,256]{2,1,0:T(2,128)(2,1)S(1)}, bf16[6,1,256]{2,1,0:T(2,128)(2,1)S(1)}, u32[]{:S(2)}, u32[]{:S(2)}) collective-permute-start(bf16[6,1,256]{2,1,0:T(2,128)(2,1)S(1)} %get-tuple-element.66), channel_id=1, source_target_pairs={{1,0},{2,1},{3,2},{4,3},{5,4},{6,5},{7,6},{8,7},{9,8},{10,9},{11,1... | collective-permute-start | bytes 9224 | tf_op jit(solution)/shard_map/ppermute | solution.py:15
  23.7 6.9 %collective-permute-done.3 = bf16[6,1,256]{2,1,0:T(2,128)(2,1)S(1)} collective-permute-done((bf16[6,1,256]{2,1,0:T(2,128)(2,1)S(1)}, bf16[6,1,256]{2,1,0:T(2,128)(2,1)S(1)}, u32[]{:S(2)}, u32[]{:S(2)}) %collective-permute-start.3) | collective-permute-done | bytes 3104 | tf_op jit(solution)/shard_map/ppermute | solution.py:15
  30.6 0.1 reshape.68
  30.7 0.1 pad_slice_fusion.18
  30.9 0.5 concatenate.36
  31.4 1.2 fusion.62
  32.9 3.1 %collective-permute-start.4 = (bf16[1,4,256]{2,1,0:T(4,128)(2,1)S(1)}, bf16[1,4,256]{2,1,0:T(4,128)(2,1)S(1)}, u32[]{:S(2)}, u32[]{:S(2)}) collective-permute-start(bf16[1,4,256]{2,1,0:T(4,128)(2,1)S(1)} %slice.338), channel_id=1, source_target_pairs={{0,32},{32,64},{64,96},{96,128},{128,160},{160,192},{192,224},{224... | collective-permute-start | bytes 6152 | tf_op jit(solution)/shard_map/ppermute | solution.py:12
  36.0 0.1 copy.111
  36.4 1.3 collective-permute-start.5
  37.7 3.0 %collective-permute-done.5 = bf16[1,4,256]{2,1,0:T(4,128)(2,1)S(1)} collective-permute-done((bf16[1,4,256]{2,1,0:T(4,128)(2,1)S(1)}, bf16[1,4,256]{2,1,0:T(4,128)(2,1)S(1)}, u32[]{:S(2)}, u32[]{:S(2)}) %collective-permute-start.5) | collective-permute-done | bytes 2080 | tf_op jit(solution)/shard_map/ppermute | solution.py:15
  40.7 3.4 %collective-permute-start.6 = (bf16[6,1,256]{2,1,0:T(2,128)(2,1)S(1)}, bf16[6,1,256]{2,1,0:T(2,128)(2,1)S(1)}, u32[]{:S(2)}, u32[]{:S(2)}) collective-permute-start(bf16[6,1,256]{2,1,0:T(2,128)(2,1)S(1)} %get-tuple-element.63), channel_id=1, source_target_pairs={{0,1},{1,2},{2,3},{3,4},{4,5},{5,6},{6,7},{7,8},{8,9},{9,10},{10,1... | collective-permute-start | bytes 9224 | tf_op jit(solution)/shard_map/ppermute | solution.py:12
  44.1 1.9 %collective-permute-start.7 = (bf16[6,1,256]{2,1,0:T(2,128)(2,1)S(1)}, bf16[6,1,256]{2,1,0:T(2,128)(2,1)S(1)}, u32[]{:S(2)}, u32[]{:S(2)}) collective-permute-start(bf16[6,1,256]{2,1,0:T(2,128)(2,1)S(1)} %get-tuple-element.64), channel_id=1, source_target_pairs={{1,0},{2,1},{3,2},{4,3},{5,4},{6,5},{7,6},{8,7},{9,8},{10,9},{11,1... | collective-permute-start | bytes 9224 | tf_op jit(solution)/shard_map/ppermute | solution.py:15
  46.1 6.9 %collective-permute-done.7 = bf16[6,1,256]{2,1,0:T(2,128)(2,1)S(1)} collective-permute-done((bf16[6,1,256]{2,1,0:T(2,128)(2,1)S(1)}, bf16[6,1,256]{2,1,0:T(2,128)(2,1)S(1)}, u32[]{:S(2)}, u32[]{:S(2)}) %collective-permute-start.7) | collective-permute-done | bytes 3104 | tf_op jit(solution)/shard_map/ppermute | solution.py:15
  53.0 0.1 reshape.72
  53.1 0.1 pad_slice_fusion
  53.3 0.5 concatenate.39
  53.8 0.3 fusion.65
  54.1 0.1 copy.114
  54.4 0.2 fusion.40
  54.6 0.2 copy.117
  54.8 0.2 reshape.89
  55.1 21.7 %all_to_all.23 = bf16[32,2,128]{2,1,0:T(2,128)(2,1)S(1)} all-to-all(bf16[32,2,128]{2,1,0:T(2,128)(2,1)S(1)} %reshape.89), channel_id=1, replica_groups=mesh['grp'=16,'dev'=32] {'dev'}, dimensions={0} | all-to-all | bytes 32768 | tf_op jit(solution)/shard_map/all_to_all | solution.py:98
  76.7 0.3 reshape.90
  77.1 0.2 copy.127
  77.3 4.3 %collective-permute-start.8 = (bf16[16,1,256]{0,2,1:T(8,128)(2,1)S(1)}, bf16[16,1,256]{0,2,1:T(8,128)(2,1)S(1)}, u32[]{:S(2)}, u32[]{:S(2)}) collective-permute-start(bf16[16,1,256]{0,2,1:T(8,128)(2,1)S(1)} %get-tuple-element.7), channel_id=1, source_target_pairs={{0,32},{32,64},{64,96},{96,128},{128,160},{160,192},{192,224},{224... | collective-permute-start | bytes 24584 | tf_op jit(solution)/shard_map/ppermute | solution.py:12
  81.6 1.5 %collective-permute-start.9 = (bf16[16,1,256]{0,2,1:T(8,128)(2,1)S(1)}, bf16[16,1,256]{0,2,1:T(8,128)(2,1)S(1)}, u32[]{:S(2)}, u32[]{:S(2)}) collective-permute-start(bf16[16,1,256]{0,2,1:T(8,128)(2,1)S(1)} %get-tuple-element.8), channel_id=1, source_target_pairs={{32,0},{64,32},{96,64},{128,96},{160,128},{192,160},{224,192},{256... | collective-permute-start | bytes 24584 | tf_op jit(solution)/shard_map/ppermute | solution.py:15
  83.1 6.0 %collective-permute-done.9 = bf16[16,1,256]{0,2,1:T(8,128)(2,1)S(1)} collective-permute-done((bf16[16,1,256]{0,2,1:T(8,128)(2,1)S(1)}, bf16[16,1,256]{0,2,1:T(8,128)(2,1)S(1)}, u32[]{:S(2)}, u32[]{:S(2)}) %collective-permute-start.9) | collective-permute-done | bytes 8224 | tf_op jit(solution)/shard_map/ppermute | solution.py:15
  89.1 0.3 select_maximum_fusion
  89.7 0.1 fusion.29
  91.7 6.1 %copy.122 = bf16[27,16,2,64,4]{1,0,4,3,2:T(8,128)(2,1)} copy(bf16[27,16,2,64,4]{1,4,3,2,0:T(4,128)(2,1)S(1)} %fusion.6) | data formatting | bytes 884736 | tf_op jit(solution)/shard_map/stack | solution.py:104
  97.9 6.1 %reshape.78 = bf16[432,2,32,2,4]{0,4,3,2,1:T(4,128)(2,1)S(1)} reshape(bf16[27,16,2,64,4]{1,0,4,3,2:T(8,128)(2,1)} %copy.122) | data formatting | bytes 884736 | tf_op jit(solution)/shard_map/reshape | solution.py:116
  104.0 0.3 copy.123
  104.2 0.3 reshape.79
  104.5 1.2 convolution_convert_fusion
  105.8 4.1 %all-to-all-start.1 = ((bf16[32,16,512]{2,1,0:T(8,128)(2,1)}), bf16[32,16,512]{2,1,0:T(8,128)(2,1)S(1)}, u32[]{:S(2)}, u32[]{:S(2)}) async-start(bf16[32,16,512]{2,1,0:T(8,128)(2,1)} %bitcast.48), calls=%async_computation.1 | async-start | bytes 1048576 | tf_op jit(solution)/shard_map/all_to_all | solution.py:28
  109.8 0.1 copy.113
  110.0 18.9 %all-to-all-done.1 = bf16[32,16,512]{2,1,0:T(8,128)(2,1)S(1)} async-done(((bf16[32,16,512]{2,1,0:T(8,128)(2,1)}), bf16[32,16,512]{2,1,0:T(8,128)(2,1)S(1)}, u32[]{:S(2)}, u32[]{:S(2)}) %all-to-all-start.1) | async-done | bytes 524320 | tf_op jit(solution)/shard_map/all_to_all | solution.py:28
  129.0 0.2 fusion.58
  129.3 0.2 reshape.82
  129.6 0.1 div.7
  129.7 0.1 reshape.83
  129.8 0.6 add_convert_fusion
  (66 shorter events, 3.4 us)
Async XLA Ops:
  0.0 129.0 %copy-start = (bf16[512,512]{1,0:T(8,128)(2,1)S(1)}, bf16[512,512]{1,0:T(8,128)(2,1)}, u32[]{:S(2)}) copy-start(bf16[512,512]{1,0:T(8,128)(2,1)} %param.11) | copy-start | bytes 1572868
  0.0 53.8 %copy-start.3 = (bf16[3,3,3,32,32]{4,3,2,1,0:T(8,128)(2,1)S(1)}, bf16[3,3,3,32,32]{4,3,2,1,0:T(8,128)(2,1)}, u32[]{:S(2)}) copy-start(bf16[3,3,3,32,32]{4,3,2,1,0:T(8,128)(2,1)} %param.8) | copy-start | bytes 165892
  0.0 54.3 %copy-start.2 = (bf16[256,512]{1,0:T(8,128)(2,1)S(1)}, bf16[256,512]{1,0:T(8,128)(2,1)}, u32[]{:S(2)}) copy-start(bf16[256,512]{1,0:T(8,128)(2,1)} %param.9) | copy-start | bytes 786436
  0.8 6.1 %collective-permute-start = (bf16[1,4,256]{2,1,0:T(4,128)(2,1)S(1)}, bf16[1,4,256]{2,1,0:T(4,128)(2,1)S(1)}, u32[]{:S(2)}, u32[]{:S(2)}) collective-permute-start(bf16[1,4,256]{2,1,0:T(4,128)(2,1)S(1)} %get-tuple-element.70), channel_id=1, source_target_pairs={{0,32},{32,64},{64,96},{96,128},{128,160},{160,192},{192,224},{224... | collective-permute-start | bytes 6152 | tf_op jit(solution)/shard_map/ppermute | solution.py:12
  5.6 5.0 %collective-permute-start.1 = (bf16[1,4,256]{2,1,0:T(4,128)(2,1)S(1)}, bf16[1,4,256]{2,1,0:T(4,128)(2,1)S(1)}, u32[]{:S(2)}, u32[]{:S(2)}) collective-permute-start(bf16[1,4,256]{2,1,0:T(4,128)(2,1)S(1)} %get-tuple-element.69), channel_id=1, source_target_pairs={{32,0},{64,32},{96,64},{128,96},{160,128},{192,160},{224,192},{256... | collective-permute-start | bytes 6152 | tf_op jit(solution)/shard_map/ppermute | solution.py:15
  10.6 13.0 %collective-permute-start.2 = (bf16[6,1,256]{2,1,0:T(2,128)(2,1)S(1)}, bf16[6,1,256]{2,1,0:T(2,128)(2,1)S(1)}, u32[]{:S(2)}, u32[]{:S(2)}) collective-permute-start(bf16[6,1,256]{2,1,0:T(2,128)(2,1)S(1)} %get-tuple-element.65), channel_id=1, source_target_pairs={{0,1},{1,2},{2,3},{3,4},{4,5},{5,6},{6,7},{7,8},{8,9},{9,10},{10,1... | collective-permute-start | bytes 9224 | tf_op jit(solution)/shard_map/ppermute | solution.py:12
  21.7 8.9 %collective-permute-start.3 = (bf16[6,1,256]{2,1,0:T(2,128)(2,1)S(1)}, bf16[6,1,256]{2,1,0:T(2,128)(2,1)S(1)}, u32[]{:S(2)}, u32[]{:S(2)}) collective-permute-start(bf16[6,1,256]{2,1,0:T(2,128)(2,1)S(1)} %get-tuple-element.66), channel_id=1, source_target_pairs={{1,0},{2,1},{3,2},{4,3},{5,4},{6,5},{7,6},{8,7},{9,8},{10,9},{11,1... | collective-permute-start | bytes 9224 | tf_op jit(solution)/shard_map/ppermute | solution.py:15
  32.9 4.8 %collective-permute-start.4 = (bf16[1,4,256]{2,1,0:T(4,128)(2,1)S(1)}, bf16[1,4,256]{2,1,0:T(4,128)(2,1)S(1)}, u32[]{:S(2)}, u32[]{:S(2)}) collective-permute-start(bf16[1,4,256]{2,1,0:T(4,128)(2,1)S(1)} %slice.338), channel_id=1, source_target_pairs={{0,32},{32,64},{64,96},{96,128},{128,160},{160,192},{192,224},{224... | collective-permute-start | bytes 6152 | tf_op jit(solution)/shard_map/ppermute | solution.py:12
  36.4 4.3 %collective-permute-start.5 = (bf16[1,4,256]{2,1,0:T(4,128)(2,1)S(1)}, bf16[1,4,256]{2,1,0:T(4,128)(2,1)S(1)}, u32[]{:S(2)}, u32[]{:S(2)}) collective-permute-start(bf16[1,4,256]{2,1,0:T(4,128)(2,1)S(1)} %slice.340), channel_id=1, source_target_pairs={{32,0},{64,32},{96,64},{128,96},{160,128},{192,160},{224,192},{256... | collective-permute-start | bytes 6152 | tf_op jit(solution)/shard_map/ppermute | solution.py:15
  40.7 5.3 %collective-permute-start.6 = (bf16[6,1,256]{2,1,0:T(2,128)(2,1)S(1)}, bf16[6,1,256]{2,1,0:T(2,128)(2,1)S(1)}, u32[]{:S(2)}, u32[]{:S(2)}) collective-permute-start(bf16[6,1,256]{2,1,0:T(2,128)(2,1)S(1)} %get-tuple-element.63), channel_id=1, source_target_pairs={{0,1},{1,2},{2,3},{3,4},{4,5},{5,6},{6,7},{7,8},{8,9},{9,10},{10,1... | collective-permute-start | bytes 9224 | tf_op jit(solution)/shard_map/ppermute | solution.py:12
  44.1 8.9 %collective-permute-start.7 = (bf16[6,1,256]{2,1,0:T(2,128)(2,1)S(1)}, bf16[6,1,256]{2,1,0:T(2,128)(2,1)S(1)}, u32[]{:S(2)}, u32[]{:S(2)}) collective-permute-start(bf16[6,1,256]{2,1,0:T(2,128)(2,1)S(1)} %get-tuple-element.64), channel_id=1, source_target_pairs={{1,0},{2,1},{3,2},{4,3},{5,4},{6,5},{7,6},{8,7},{9,8},{10,9},{11,1... | collective-permute-start | bytes 9224 | tf_op jit(solution)/shard_map/ppermute | solution.py:15
  77.3 5.8 %collective-permute-start.8 = (bf16[16,1,256]{0,2,1:T(8,128)(2,1)S(1)}, bf16[16,1,256]{0,2,1:T(8,128)(2,1)S(1)}, u32[]{:S(2)}, u32[]{:S(2)}) collective-permute-start(bf16[16,1,256]{0,2,1:T(8,128)(2,1)S(1)} %get-tuple-element.7), channel_id=1, source_target_pairs={{0,32},{32,64},{64,96},{96,128},{128,160},{160,192},{192,224},{224... | collective-permute-start | bytes 24584 | tf_op jit(solution)/shard_map/ppermute | solution.py:12
  81.6 7.5 %collective-permute-start.9 = (bf16[16,1,256]{0,2,1:T(8,128)(2,1)S(1)}, bf16[16,1,256]{0,2,1:T(8,128)(2,1)S(1)}, u32[]{:S(2)}, u32[]{:S(2)}) collective-permute-start(bf16[16,1,256]{0,2,1:T(8,128)(2,1)S(1)} %get-tuple-element.8), channel_id=1, source_target_pairs={{32,0},{64,32},{96,64},{128,96},{160,128},{192,160},{224,192},{256... | collective-permute-start | bytes 24584 | tf_op jit(solution)/shard_map/ppermute | solution.py:15
  97.9 6.7 %copy-start.1 = (bf16[3,3,3,16,512]{4,3,2,1,0:T(8,128)(2,1)S(1)}, bf16[3,3,3,16,512]{4,3,2,1,0:T(8,128)(2,1)}, u32[]{:S(2)}) copy-start(bf16[3,3,3,16,512]{4,3,2,1,0:T(8,128)(2,1)} %param.10) | copy-start | bytes 1327108
  105.8 23.2 %all-to-all-start.1 = ((bf16[32,16,512]{2,1,0:T(8,128)(2,1)}), bf16[32,16,512]{2,1,0:T(8,128)(2,1)S(1)}, u32[]{:S(2)}, u32[]{:S(2)}) async-start(bf16[32,16,512]{2,1,0:T(8,128)(2,1)} %bitcast.48), calls=%async_computation.1 | async-start | bytes 1048576 | tf_op jit(solution)/shard_map/all_to_all | solution.py:28
where the time goes:
time: 132 us; the launch traced here: 130 us
  waiting for transfers between devices  44.7 us (34%)
  starting transfers between devices  38.7 us (29%)
  blocking collectives  21.7 us (16%)
  local copies, waits for them, and re-layouts  20.5 us (16%)
  matrix products  3.19 us (2%)
  other arithmetic  1.33 us (1%)
    ppermute x5, starting transfers between devices, with_halo(): lax.ppermute(lax.slice_in_dim(block, block.shape[dim] - width, None, axis...  26.7 us
    ppermute x5, waiting for transfers between devices, with_halo(): lax.ppermute(lax.slice_in_dim(block, 0, width, axis=dim), axis, backward)  25.8 us
    all_to_all x1, blocking collectives, on_device(): lax.all_to_all(spread, 'dev', split_axis=0, concat_axis=2, tiled=True)  21.7 us
    all_to_all x1, waiting for transfers between devices, sum_at_owner(): pieces = lax.all_to_all(in_blocks(x, dim, count), axis, 0, 0, tiled=True)  18.9 us
    ppermute x5, starting transfers between devices, with_halo(): lax.ppermute(lax.slice_in_dim(block, 0, width, axis=dim), axis, backward)  7.9 us
    another operation x2, local copies, waits for them, and re-layouts, on_device(): jnp.stack([rimmed[:, along_x:along_x + coarse_x, along_y:along_y + span_y...  6.21 us
    reshape x1, local copies, waits for them, and re-layouts, on_device(): columns.reshape(27 * in_block, coarse_x, devices, coarse_y, coarse_z)  6.08 us
    all_to_all x1, starting transfers between devices, sum_at_owner(): pieces = lax.all_to_all(in_blocks(x, dim, count), axis, 0, 0, tiled=True)  4.05 us
  transfers between devices with their start and end apart: 11, of which 6 were waited for; matrix products, arithmetic and copies ran while one was open for 1% of the time, Pallas kernels for 0%

commit v1 on v0

v1 whole, which is shorter than its diff:
```python
import functools

import jax
import jax.numpy as jnp
from jax import lax
from jax.experimental import pallas as pl
from jax.experimental.pallas import tpu as pltpu
from jax.sharding import PartitionSpec as P

F32 = jnp.float32
BF16 = jnp.bfloat16
MESH = pl.DeviceIdType.MESH
BANDS = [(zi, zo) for zo in range(4) for zi in range(4) if abs(zi - zo) <= 1]
GAPS = [(zi, zo) for zo in range(4) for zi in range(4) if abs(zi - zo) > 1]


def gelu(v):
    return 0.5 * v * (1.0 + lax.erf(v * 0.7071067811865476))


def dot(a, b):
    return jnp.dot(a, b, preferred_element_type=F32)


def iota(shape, dim):
    return lax.broadcasted_iota(jnp.int32, shape, dim)


def one_hot(mask):
    return jnp.where(mask, 1.0, 0.0).astype(BF16)


def band_weights(w_ref, t_ref):
    spread = one_hot((iota((32, 256), 1) & 31) == iota((32, 256), 0))
    lane_z = iota((32, 256), 1) >> 5

    def body(tap, carry):
        w0 = dot(w_ref[tap, 0], spread)
        w1 = dot(w_ref[tap, 1], spread)
        w2 = dot(w_ref[tap, 2], spread)
        for zi in range(8):
            rows = jnp.where(
                lane_z == zi,
                w1,
                jnp.where(lane_z == zi - 1, w2, jnp.where(lane_z == zi + 1, w0, 0.0)),
            )
            t_ref[tap, zi * 32 : zi * 32 + 32, :] = rows.astype(BF16)
        return carry

    lax.fori_loop(0, 9, body, 0)


def kernel(
    groups, devices,
    vol, w1, w2, wl, wc, wu,
    out,
    blocks, w1_v, w2_v, wl_v, wu_v, t1, t2, tc, wide, first, skip_p, send, recv, flat, cols, sums, parts, shares,
    load_sem, own_sem, halo_s, halo_r, wc_s, wc_r, a2a_s, a2a_r, rs_s, rs_r,
):
    g = lax.axis_index("grp")
    d = lax.axis_index("dev")
    half = devices // 2
    e = d // 2
    core = d - 2 * e
    lanes = wl.shape[1]

    barrier = pltpu.get_barrier_semaphore()

    def greet(off, carry):
        pl.semaphore_signal(
            barrier, inc=1, device_id=(g, lax.rem(d + off, devices)), device_id_type=MESH
        )
        return carry

    lax.fori_loop(1, devices, greet, 0)
    for dx in (-1, 1):
        for dy in (-1, 0, 1):
            pl.semaphore_signal(
                barrier, inc=1,
                device_id=(lax.rem(g + dx + groups, groups), lax.rem(d + dy + devices, devices)),
                device_id_type=MESH,
            )

    loads = [
        pltpu.make_async_copy(src, dst, load_sem.at[i])
        for i, (src, dst) in enumerate(
            [(w1, w1_v), (w2, w2_v), (wl, wl_v), (wu, wu_v), (vol, blocks.at[4])]
        )
    ]
    for c in loads:
        c.start()
    own = []
    for i, (zi, zo) in enumerate(BANDS):
        own.append(
            pltpu.make_async_copy(
                wc.at[:, zi - zo + 1],
                tc.at[:, zi, core, :, pl.ds(zo * lanes, lanes)],
                own_sem.at[i],
            )
        )
        own[-1].start()

    pl.semaphore_wait(barrier, devices - 1 + 6)

    halo = []
    for dx in (-1, 0, 1):
        for dy in (-1, 0, 1):
            if dx == 0 and dy == 0:
                continue
            slot = (1 - dx) * 3 + 1 - dy
            halo.append(
                pltpu.make_async_remote_copy(
                    src_ref=vol,
                    dst_ref=blocks.at[slot],
                    send_sem=halo_s.at[slot],
                    recv_sem=halo_r.at[slot],
                    device_id=(
                        lax.rem(g + dx + groups, groups),
                        lax.rem(d + dy + devices, devices),
                    ),
                    device_id_type=MESH,
                )
            )
            halo[-1].start()
    twin = []
    for i, (zi, zo) in enumerate(BANDS):
        twin.append(
            pltpu.make_async_remote_copy(
                src_ref=wc.at[:, zi - zo + 1],
                dst_ref=tc.at[:, zi, core, :, pl.ds(zo * lanes, lanes)],
                send_sem=wc_s.at[i],
                recv_sem=wc_r.at[i],
                device_id=(g, d + 1 - 2 * core),
                device_id_type=MESH,
            )
        )
        twin[-1].start()

    for zi, zo in GAPS:
        tc[:, zi, :, :, zo * lanes : zo * lanes + lanes] = jnp.zeros((9, 2, 16, lanes), BF16)
    wide[96:104] = jnp.zeros((8, 256), F32)
    first[80:88] = jnp.zeros((8, 256), F32)
    flat[0:8] = jnp.zeros((8, 128), F32)
    flat[8 + 8 * devices : 16 + 8 * devices] = jnp.zeros((8, 128), F32)
    loads[0].wait()
    band_weights(w1_v, t1)
    loads[1].wait()
    band_weights(w2_v, t2)

    row, col = iota((96, 144), 0), iota((96, 144), 1)
    slot = col >> 4
    sx = (slot >= 3).astype(jnp.int32) + (slot >= 6).astype(jnp.int32)
    sy = slot - 3 * sx
    fits = (sx * 4 + ((col >> 2) & 3) == (row >> 3)) & (sy * 4 + (col & 3) - 2 == (row & 7))
    gx, gy = g - 1 + sx, d - 1 + sy
    fits = fits & (gx >= 0) & (gx < groups) & (gy >= 0) & (gy < devices)
    place = one_hot(fits)

    for c in loads[2:]:
        c.wait()
    for c in halo:
        c.wait_recv()
    wide[0:96] = dot(place, blocks[...].reshape(144, 256))

    total = jnp.zeros((80, 256), F32)
    for tap in range(9):
        off = (tap // 3) * 8 + tap % 3
        total += dot(wide[off : off + 80].astype(BF16), t1[tap])
    rows = iota((80, 256), 0)
    fx, fy = 4 * g - 3 + (rows >> 3), 4 * d - 1 + (rows & 7)
    inside = (fx >= 0) & (fx < 4 * groups) & (fy >= 0) & (fy < 4 * devices)
    act = gelu(total).astype(BF16).astype(F32)
    first[0:80] = jnp.where(inside, act, 0.0)

    total = jnp.zeros((64, 256), F32)
    for tap in range(9):
        off = (tap // 3) * 8 + tap % 3
        total += dot(first[off : off + 64].astype(BF16), t2[tap])
    skip = gelu(total).astype(BF16)

    row, col = iota((32, 64), 0), iota((32, 64), 1)
    ci = (row >> 1) & 3
    fits = (2 * ci + (row >> 4) == (col >> 3)) & (2 * (row & 1) + ((row >> 3) & 1) == (col & 7))
    cx = 2 * g - 1 + ci
    fits = fits & (cx >= 0) & (cx < 2 * groups)
    moved = dot(one_hot(fits), skip)
    skip_p[...] = moved
    stacked = jnp.concatenate(
        [
            jnp.concatenate(
                [moved[ab * 8 : ab * 8 + 8, k * 64 : k * 64 + 64] for ab in range(4)], axis=1
            )
            for k in range(4)
        ],
        axis=0,
    )
    lifted = gelu(dot(stacked.astype(BF16), wl_v[...]))
    for t in range(half):
        send[t] = jnp.concatenate(
            [lifted[k * 8 : k * 8 + 8, t * 32 : t * 32 + 32] for k in range(4)], axis=1
        ).astype(BF16)

    def spread_copy(off):
        to = lax.rem(d + off, devices)
        frm = lax.rem(d + devices - off, devices)
        return to, frm

    def spread_start(off, carry):
        to = lax.rem(d + off, devices)
        pltpu.make_async_remote_copy(
            src_ref=send.at[to // 2],
            dst_ref=recv.at[d],
            send_sem=a2a_s.at[to],
            recv_sem=a2a_r.at[d],
            device_id=(g, to),
            device_id_type=MESH,
        ).start()
        return carry

    lax.fori_loop(1, devices, spread_start, 0)
    recv[d] = send[e]
    for c in own:
        c.wait()
    for c in twin:
        c.wait_recv()

    def spread_wait(off, carry):
        frm = lax.rem(d + off, devices)
        pltpu.make_async_remote_copy(
            src_ref=send.at[frm // 2],
            dst_ref=recv.at[frm],
            send_sem=a2a_s.at[frm],
            recv_sem=a2a_r.at[frm],
            device_id=(g, frm),
            device_id_type=MESH,
        ).wait_recv()
        return carry

    lax.fori_loop(1, devices, spread_wait, 0)

    flat[8 : 8 + 8 * devices] = recv[...].astype(F32).reshape(8 * devices, 128)
    for xx in range(4):
        for yb in range(4):
            ds, y = ((-1, 1), (0, 0), (0, 1), (1, 0))[yb]
            piece = flat[pl.ds(8 + 8 * core + 8 * ds + 2 * xx + y, half, stride=16), :].astype(BF16)
            for a in range(3):
                for b in range(3):
                    x, yy = xx - a, yb - b
                    if 0 <= x < 2 and 0 <= yy < 2:
                        at, tap = (2 * x + yy) * half, 3 * a + b
                        cols[at : at + half, tap * 128 : tap * 128 + 128] = piece

    lhs = cols[...]
    for z in range(4):
        got = dot(lhs, tc[:, :, :, :, z * lanes : z * lanes + lanes].reshape(1152, lanes))
        for q in range(4):
            for lt in range(lanes // 128):
                sums[lt, pl.ds(4 * z + q, half, stride=16), :] = got[
                    q * half : q * half + half, lt * 128 : lt * 128 + 128
                ]
    for lt in range(lanes // 128):
        parts[:, :, lt * 128 : lt * 128 + 128] = sums[lt].reshape(half, 16, 128).astype(BF16)

    def share_start(off, carry):
        to = lax.rem(e + off, half)
        pltpu.make_async_remote_copy(
            src_ref=parts.at[to],
            dst_ref=shares.at[e],
            send_sem=rs_s.at[to],
            recv_sem=rs_r.at[e],
            device_id=(g, 2 * to + core),
            device_id_type=MESH,
        ).start()
        return carry

    lax.fori_loop(1, half, share_start, 0)
    shares[e] = parts[e]

    def share_copy(off):
        frm = lax.rem(e + off, half)
        return pltpu.make_async_remote_copy(
            src_ref=parts.at[frm],
            dst_ref=shares.at[frm],
            send_sem=rs_s.at[frm],
            recv_sem=rs_r.at[frm],
            device_id=(g, 2 * frm + core),
            device_id_type=MESH,
        )

    def share_wait(off, carry):
        share_copy(off).wait_recv()
        return carry

    lax.fori_loop(1, half, share_wait, 0)
    total = shares[0].astype(F32)
    for t in range(1, half):
        total += shares[t].astype(F32)

    coarse = gelu(total).astype(BF16)
    upper = dot(coarse, wu_v[...])

    def expand(base):
        return jnp.concatenate(
            [
                jnp.concatenate(
                    [
                        upper[4 * k : 4 * k + 4, base + ab * 64 : base + ab * 64 + 64]
                        for k in range(4)
                    ],
                    axis=1,
                )
                for ab in range(4)
            ],
            axis=0,
        )

    gate, value = expand(0), expand(256)
    mine = jnp.concatenate([skip_p[ab * 8 + 2 : ab * 8 + 6] for ab in range(4)], axis=0)
    mixed = (mine * jax.nn.sigmoid(gate) + value).astype(BF16)
    row, col = iota((16, 16), 0), iota((16, 16), 1)
    fits = ((row >> 2) == 2 * ((col >> 1) & 1) + (col >> 3)) & (
        (row & 3) == 2 * (col & 1) + ((col >> 2) & 1)
    )
    out[...] = dot(one_hot(fits), mixed).astype(BF16)

    for c in halo:
        c.wait_send()
    for c in twin:
        c.wait_send()

    def spread_sent(off, carry):
        to = lax.rem(d + off, devices)
        pltpu.make_async_remote_copy(
            src_ref=send.at[to // 2],
            dst_ref=recv.at[d],
            send_sem=a2a_s.at[to],
            recv_sem=a2a_r.at[d],
            device_id=(g, to),
            device_id_type=MESH,
        ).wait_send()
        return carry

    lax.fori_loop(1, devices, spread_sent, 0)

    def share_sent(off, carry):
        share_copy(off).wait_send()
        return carry

    lax.fori_loop(1, half, share_sent, 0)


def on_device(groups, devices, volume, w_first, w_second, w_lift, w_coarse, w_up):
    half = devices // 2
    wide = w_up.shape[0]
    anywhere = pl.BlockSpec(memory_space=pl.ANY)
    dma = pltpu.SemaphoreType.DMA
    result = pl.pallas_call(
        functools.partial(kernel, groups, devices),
        out_shape=jax.ShapeDtypeStruct((16, 256), BF16),
        in_specs=[anywhere] * 6,
        out_specs=pl.BlockSpec(memory_space=pltpu.VMEM),
        scratch_shapes=[
            pltpu.VMEM((9, 16, 256), BF16),
            pltpu.VMEM((9, 3, 32, 32), BF16),
            pltpu.VMEM((9, 3, 32, 32), BF16),
            pltpu.VMEM((256, wide), BF16),
            pltpu.VMEM((wide, 512), BF16),
            pltpu.VMEM((9, 256, 256), BF16),
            pltpu.VMEM((9, 256, 256), BF16),
            pltpu.VMEM((9, 4, 2, 16, 4 * wide), BF16),
            pltpu.VMEM((104, 256), F32),
            pltpu.VMEM((88, 256), F32),
            pltpu.VMEM((32, 256), F32),
            pltpu.VMEM((half, 8, 128), BF16),
            pltpu.VMEM((devices, 8, 128), BF16),
            pltpu.VMEM((8 * devices + 16, 128), F32),
            pltpu.VMEM((4 * half, 1152), BF16),
            pltpu.VMEM((wide // 128, 16 * half, 128), F32),
            pltpu.VMEM((half, 16, wide), BF16),
            pltpu.VMEM((half, 16, wide), BF16),
            dma((5,)),
            dma((10,)),
            dma((9,)),
            dma((9,)),
            dma((10,)),
            dma((10,)),
            dma((devices,)),
            dma((devices,)),
            dma((half,)),
            dma((half,)),
        ],
        compiler_params=pltpu.CompilerParams(
            collective_id=0, has_side_effects=True, vmem_limit_bytes=48 * 1024 * 1024
        ),
    )(
        volume.reshape(16, 256),
        w_first.reshape(9, 3, 32, 32),
        w_second.reshape(9, 3, 32, 32),
        w_lift,
        w_coarse.reshape(9, 3, 16, wide),
        w_up,
    )
    return result.reshape(4, 4, 256)


def solution(mesh):
    return jax.shard_map(
        functools.partial(on_device, mesh.shape["grp"], mesh.shape["dev"]),
        mesh=mesh,
        in_specs=(P("grp", "dev", None), P(), P(), P(), P(None, None, None, "dev", None), P()),
        out_specs=P("grp", "dev", None),
        check_vma=False,
    )
```

time: 132 us -> 52.7 us (0.40)
  Pallas kernels: 0 us -> 46.2 us
  waiting for transfers between devices: 44.7 us -> 0 us
  starting transfers between devices: 38.7 us -> 0 us
  blocking collectives: 21.7 us -> 0 us
  local copies, waits for them, and re-layouts: 20.5 us -> 6.19 us
  matrix products: 3.19 us -> 0 us
  other arithmetic: 1.33 us -> 0 us
    pallas_call x0 -> x1, Pallas kernels: none -> 46.2 us  [on_device(): pl.pallas_call(functools.partial(kernel, groups, devices), out_shape=jax....]
    ppermute x10 -> x0, starting transfers between devices: 34.6 us -> none  [the longest x5 26.7 us: with_halo(): lax.ppermute(lax.slice_in_dim(block, block.shape[dim] - width, None, axis...]
    ppermute x10 -> x0, waiting for transfers between devices: 25.8 us -> none  [the longest x5 25.8 us: with_halo(): lax.ppermute(lax.slice_in_dim(block, 0, width, axis=dim), axis, backward)]
    all_to_all x1 -> x0, blocking collectives: 21.7 us -> none  [on_device(): lax.all_to_all(spread, 'dev', split_axis=0, concat_axis=2, tiled=True)]
    all_to_all x1 -> x0, waiting for transfers between devices: 18.9 us -> none  [sum_at_owner(): pieces = lax.all_to_all(in_blocks(x, dim, count), axis, 0, 0, tiled=True)]
    another operation x2 -> x0, local copies, waits for them, and re-layouts: 6.21 us -> none  [on_device(): jnp.stack([rimmed[:, along_x:along_x + coarse_x, along_y:along_y + span_y...]
    reshape x11 -> x2, local copies, waits for them, and re-layouts: 7.24 us -> 1.31 us  [the longest x1 0.71 us: on_device(): volume.reshape(16, 256)]
    all_to_all x1 -> x0, starting transfers between devices: 4.05 us -> none  [sum_at_owner(): pieces = lax.all_to_all(in_blocks(x, dim, count), axis, 0, 0, tiled=True)]
  transfers between devices with their start and end apart: 11 -> 0, of which waited for: 6 -> 0; matrix products, arithmetic and copies ran while one was open for 1% -> 0% of each run, Pallas kernels for 0% -> 0%
where the time goes in v1:
time: 52.7 us; the launch traced here: 52.4 us
  Pallas kernels  46.2 us (88%)
  local copies, waits for them, and re-layouts  6.19 us (12%)
    pallas_call x1, Pallas kernels, on_device(): pl.pallas_call(functools.partial(kernel, groups, devices), out_shape=jax....  46.2 us
    unnamed x10, local copies, waits for them, and re-layouts  4.87 us

profile of v1, /device:TPU:1, one launch (start us, length us, event | category | flops | bytes accessed | tf_op | source)
XLA Modules:
  0.0 52.4 jit_solution(10450546552981715768)
XLA Ops:
  0.0 0.7 %reshape.15.vol = bf16[16,256]{1,0:T(8,128)(2,1)S(1)} reshape(bf16[4,4,256]{2,1,0:T(4,128)(2,1)} %param.6) | data formatting | bytes 16384 | tf_op jit(solution)/shard_map/reshape | solution.py:396
  0.7 0.0 copy-start
  0.7 1.0 %copy-done = bf16[512,512]{1,0:T(8,128)(2,1)S(1)} copy-done((bf16[512,512]{1,0:T(8,128)(2,1)S(1)}, bf16[512,512]{1,0:T(8,128)(2,1)}, u32[]{:S(2)}) %copy-start) | copy-done | bytes 524312
  1.7 0.0 copy-start.1
  1.8 1.0 %copy-done.1 = bf16[3,3,3,16,512]{4,3,2,1,0:T(8,128)(2,1)S(1)} copy-done((bf16[3,3,3,16,512]{4,3,2,1,0:T(8,128)(2,1)S(1)}, bf16[3,3,3,16,512]{4,3,2,1,0:T(8,128)(2,1)}, u32[]{:S(2)}) %copy-start.1) | copy-done | bytes 442392
  2.8 0.0 copy-start.2
  2.8 0.9 %copy-done.2 = bf16[256,512]{1,0:T(8,128)(2,1)S(1)} copy-done((bf16[256,512]{1,0:T(8,128)(2,1)S(1)}, bf16[256,512]{1,0:T(8,128)(2,1)}, u32[]{:S(2)}) %copy-start.2) | copy-done | bytes 262168
  3.7 0.0 copy-start.3
  3.7 0.9 %copy-done.3 = bf16[3,3,3,32,32]{4,3,2,1,0:T(8,128)(2,1)S(1)} copy-done((bf16[3,3,3,32,32]{4,3,2,1,0:T(8,128)(2,1)S(1)}, bf16[3,3,3,32,32]{4,3,2,1,0:T(8,128)(2,1)}, u32[]{:S(2)}) %copy-start.3) | copy-done | bytes 55320
  4.6 0.0 copy-start.4
  4.7 0.9 %copy-done.4 = bf16[3,3,3,32,32]{4,3,2,1,0:T(8,128)(2,1)S(1)} copy-done((bf16[3,3,3,32,32]{4,3,2,1,0:T(8,128)(2,1)S(1)}, bf16[3,3,3,32,32]{4,3,2,1,0:T(8,128)(2,1)}, u32[]{:S(2)}) %copy-start.4) | copy-done | bytes 55320
  5.6 46.2 %shard_map.64 = bf16[16,256]{1,0:T(8,128)(2,1)S(1)} custom-call(bf16[16,256]{1,0:T(8,128)(2,1)S(1)} %reshape.15.vol, bf16[9,3,32,32]{3,2,1,0:T(8,128)(2,1)S(1)} %bitcast.4, bf16[9,3,32,32]{3,2,1,0:T(8,128)(2,1)S(1)} %bitcast.5, bf16[256,512]{1,0:T(8,128)(2,1)S(1)} %copy-done.2, bf16[9,3,16,512]{3,2,1,0:T(8,128)(2,1)S(1)} %bitcast.3, bf16[512,512]{1,0:T(8,128)(2,1)S(1)} %copy-done), custom_call_target="tpu_custom_call" | custom-call | tf_op jit(solution)/shard_map/pallas_call | solution.py:357
  51.8 0.6 %reshape.19 = bf16[4,4,256]{2,1,0:T(4,128)(2,1)} reshape(bf16[16,256]{1,0:T(8,128)(2,1)S(1)} %shard_map.64) | data formatting | bytes 16384 | tf_op jit(solution)/shard_map/reshape | solution.py:403
Async XLA Ops:
  0.7 1.0 %copy-start = (bf16[512,512]{1,0:T(8,128)(2,1)S(1)}, bf16[512,512]{1,0:T(8,128)(2,1)}, u32[]{:S(2)}) copy-start(bf16[512,512]{1,0:T(8,128)(2,1)} %wu.1) | copy-start | bytes 1572868
  1.7 1.0 %copy-start.1 = (bf16[3,3,3,16,512]{4,3,2,1,0:T(8,128)(2,1)S(1)}, bf16[3,3,3,16,512]{4,3,2,1,0:T(8,128)(2,1)}, u32[]{:S(2)}) copy-start(bf16[3,3,3,16,512]{4,3,2,1,0:T(8,128)(2,1)} %param.10) | copy-start | bytes 1327108
  2.8 0.9 %copy-start.2 = (bf16[256,512]{1,0:T(8,128)(2,1)S(1)}, bf16[256,512]{1,0:T(8,128)(2,1)}, u32[]{:S(2)}) copy-start(bf16[256,512]{1,0:T(8,128)(2,1)} %wl.1) | copy-start | bytes 786436
  3.7 0.9 %copy-start.3 = (bf16[3,3,3,32,32]{4,3,2,1,0:T(8,128)(2,1)S(1)}, bf16[3,3,3,32,32]{4,3,2,1,0:T(8,128)(2,1)}, u32[]{:S(2)}) copy-start(bf16[3,3,3,32,32]{4,3,2,1,0:T(8,128)(2,1)} %param.7) | copy-start | bytes 165892
  4.6 0.9 %copy-start.4 = (bf16[3,3,3,32,32]{4,3,2,1,0:T(8,128)(2,1)S(1)}, bf16[3,3,3,32,32]{4,3,2,1,0:T(8,128)(2,1)}, u32[]{:S(2)}) copy-start(bf16[3,3,3,32,32]{4,3,2,1,0:T(8,128)(2,1)} %param.8) | copy-start | bytes 165892

commit v2 on v1

--- a/solution.py
+++ b/solution.py
@@ -59,27 +59,34 @@
 ):
     g = lax.axis_index("grp")
     d = lax.axis_index("dev")
-    half = devices // 2
+    half, ring = devices // 2, devices // 4
     e = d // 2
     core = d - 2 * e
     lanes = wl.shape[1]
 
     barrier = pltpu.get_barrier_semaphore()
 
-    def greet(off, carry):
-        pl.semaphore_signal(
-            barrier, inc=1, device_id=(g, lax.rem(d + off, devices)), device_id_type=MESH
-        )
-        return carry
-
-    lax.fori_loop(1, devices, greet, 0)
-    for dx in (-1, 1):
-        for dy in (-1, 0, 1):
-            pl.semaphore_signal(
-                barrier, inc=1,
-                device_id=(lax.rem(g + dx + groups, groups), lax.rem(d + dy + devices, devices)),
-                device_id_type=MESH,
-            )
+    y, zh = e // 2, e - 2 * (e // 2)
+
+    def member(dy, other_zh, other_core):
+        to_y = lax.rem(y + dy + ring, ring)
+        to_zh = 1 - zh if other_zh else zh
+        to_core = 1 - core if other_core else core
+        return (to_y * 2 + to_zh) * 2 + to_core
+
+    steps = [ring // 2]
+    for k in range(ring // 2 - 1, 0, -1):
+        steps += [k, -k]
+    members = [(k, a, b) for k in steps + [0] for a in (1, 0) for b in (0, 1)][:-2] + [(0, 0, 1)]
+
+    def neighbour(dx, dy):
+        return lax.rem(g + dx + groups, groups), lax.rem(d + dy + devices, devices)
+
+    beside = [(dx, dy) for dx in (-1, 1) for dy in (-1, 1, 0)]
+    for dx, dy in beside:
+        pl.semaphore_signal(barrier, inc=1, device_id=neighbour(dx, dy), device_id_type=MESH)
+    for m in members:
+        pl.semaphore_signal(barrier, inc=1, device_id=(g, member(*m)), device_id_type=MESH)
 
     loads = [
         pltpu.make_async_copy(src, dst, load_sem.at[i])
@@ -103,25 +110,19 @@
     pl.semaphore_wait(barrier, devices - 1 + 6)
 
     halo = []
-    for dx in (-1, 0, 1):
-        for dy in (-1, 0, 1):
-            if dx == 0 and dy == 0:
-                continue
-            slot = (1 - dx) * 3 + 1 - dy
-            halo.append(
-                pltpu.make_async_remote_copy(
-                    src_ref=vol,
-                    dst_ref=blocks.at[slot],
-                    send_sem=halo_s.at[slot],
-                    recv_sem=halo_r.at[slot],
-                    device_id=(
-                        lax.rem(g + dx + groups, groups),
-                        lax.rem(d + dy + devices, devices),
-                    ),
-                    device_id_type=MESH,
-                )
-            )
-            halo[-1].start()
+    for dx, dy in [(0, -1), (0, 1)] + beside:
+        slot = (1 - dx) * 3 + 1 - dy
+        halo.append(
+            pltpu.make_async_remote_copy(
+                src_ref=vol,
+                dst_ref=blocks.at[slot],
+                send_sem=halo_s.at[slot],
+                recv_sem=halo_r.at[slot],
+                device_id=neighbour(dx, dy),
+                device_id_type=MESH,
+            )
+        )
+        halo[-1].start()
     twin = []
     for i, (zi, zo) in enumerate(BANDS):
         twin.append(
@@ -200,24 +201,19 @@
             [lifted[k * 8 : k * 8 + 8, t * 32 : t * 32 + 32] for k in range(4)], axis=1
         ).astype(BF16)
 
-    def spread_copy(off):
-        to = lax.rem(d + off, devices)
-        frm = lax.rem(d + devices - off, devices)
-        return to, frm
-
-    def spread_start(off, carry):
-        to = lax.rem(d + off, devices)
-        pltpu.make_async_remote_copy(
+    def spread(m):
+        to = member(*m)
+        return pltpu.make_async_remote_copy(
             src_ref=send.at[to // 2],
             dst_ref=recv.at[d],
             send_sem=a2a_s.at[to],
             recv_sem=a2a_r.at[d],
             device_id=(g, to),
             device_id_type=MESH,
-        ).start()
-        return carry
-
-    lax.fori_loop(1, devices, spread_start, 0)
+        )
+
+    for m in members:
+        spread(m).start()
     recv[d] = send[e]
     for c in own:
         c.wait()
@@ -241,8 +237,8 @@
     flat[8 : 8 + 8 * devices] = recv[...].astype(F32).reshape(8 * devices, 128)
     for xx in range(4):
         for yb in range(4):
-            ds, y = ((-1, 1), (0, 0), (0, 1), (1, 0))[yb]
-            piece = flat[pl.ds(8 + 8 * core + 8 * ds + 2 * xx + y, half, stride=16), :].astype(BF16)
+            ds, ly = ((-1, 1), (0, 0), (0, 1), (1, 0))[yb]
+            piece = flat[pl.ds(8 + 8 * core + 8 * ds + 2 * xx + ly, half, stride=16), :].astype(BF16)
             for a in range(3):
                 for b in range(3):
                     x, yy = xx - a, yb - b
@@ -261,19 +257,20 @@
     for lt in range(lanes // 128):
         parts[:, :, lt * 128 : lt * 128 + 128] = sums[lt].reshape(half, 16, 128).astype(BF16)
 
-    def share_start(off, carry):
-        to = lax.rem(e + off, half)
-        pltpu.make_async_remote_copy(
+    def share(to):
+        return pltpu.make_async_remote_copy(
             src_ref=parts.at[to],
             dst_ref=shares.at[e],
             send_sem=rs_s.at[to],
             recv_sem=rs_r.at[e],
             device_id=(g, 2 * to + core),
             device_id_type=MESH,
-        ).start()
-        return carry
-
-    lax.fori_loop(1, half, share_start, 0)
+        )
+
+    owners = [2 * lax.rem(y + k + ring, ring) for k in steps]
+    owners = owners + [2 * y + 1 - zh] + [to + 1 for to in owners]
+    for to in owners:
+        share(to).start()
     shares[e] = parts[e]
 
     def share_copy(off):
@@ -328,36 +325,21 @@
     for c in twin:
         c.wait_send()
 
-    def spread_sent(off, carry):
-        to = lax.rem(d + off, devices)
-        pltpu.make_async_remote_copy(
-            src_ref=send.at[to // 2],
-            dst_ref=recv.at[d],
-            send_sem=a2a_s.at[to],
-            recv_sem=a2a_r.at[d],
-            device_id=(g, to),
-            device_id_type=MESH,
-        ).wait_send()
-        return carry
-
-    lax.fori_loop(1, devices, spread_sent, 0)
-
-    def share_sent(off, carry):
-        share_copy(off).wait_send()
-        return carry
-
-    lax.fori_loop(1, half, share_sent, 0)
+    for m in members:
+        spread(m).wait_send()
+    for to in owners:
+        share(to).wait_send()
 
 
 def on_device(groups, devices, volume, w_first, w_second, w_lift, w_coarse, w_up):
     half = devices // 2
     wide = w_up.shape[0]
-    anywhere = pl.BlockSpec(memory_space=pl.ANY)
+    in_hbm = pl.BlockSpec(memory_space=pltpu.HBM)
     dma = pltpu.SemaphoreType.DMA
     result = pl.pallas_call(
         functools.partial(kernel, groups, devices),
         out_shape=jax.ShapeDtypeStruct((16, 256), BF16),
-        in_specs=[anywhere] * 6,
+        in_specs=[pl.BlockSpec(memory_space=pl.ANY)] + [in_hbm] * 5,
         out_specs=pl.BlockSpec(memory_space=pltpu.VMEM),
         scratch_shapes=[
             pltpu.VMEM((9, 16, 256), BF16),
@@ -390,7 +372,7 @@
             dma((half,)),
         ],
         compiler_params=pltpu.CompilerParams(
-            collective_id=0, has_side_effects=True, vmem_limit_bytes=48 * 1024 * 1024
+            collective_id=0, has_side_effects=True, vmem_limit_bytes=56 * 1024 * 1024
         ),
     )(
         volume.reshape(16, 256),

time: 52.7 us -> 45.3 us (0.86)
  Pallas kernels: 46.2 us -> 42.4 us
  local copies, waits for them, and re-layouts: 6.19 us -> 2.61 us
    unnamed x10 -> x0, local copies, waits for them, and re-layouts: 4.87 us -> none
    pallas_call x1, Pallas kernels: 46.2 us -> 42.4 us  [on_device(): pl.pallas_call(functools.partial(kernel, groups, devices), out_shape=jax....]
    reshape x1, local copies, waits for them, and re-layouts: 0.61 us -> 1.3 us  [on_device(): return result.reshape(4, 4, 256)]
    reshape x1, local copies, waits for them, and re-layouts: 0.71 us -> 1.3 us  [on_device(): volume.reshape(16, 256)]
where the time goes in v2:
time: 45.3 us; the launch traced here: 45 us
  Pallas kernels  42.4 us (94%)
  local copies, waits for them, and re-layouts  2.61 us (6%)
    pallas_call x1, Pallas kernels, on_device(): pl.pallas_call(functools.partial(kernel, groups, devices), out_shape=jax....  42.4 us
    reshape x1, local copies, waits for them, and re-layouts, on_device(): return result.reshape(4, 4, 256)  1.3 us
    reshape x1, local copies, waits for them, and re-layouts, on_device(): volume.reshape(16, 256)  1.3 us

profile of v2, /device:TPU:1, one launch (start us, length us, event | category | flops | bytes accessed | tf_op | source)
XLA Modules:
  0.0 45.0 jit_solution(15650577916015579344)
XLA Ops:
  0.0 1.3 %reshape.15.vol = bf16[16,256]{1,0:T(8,128)(2,1)} reshape(bf16[4,4,256]{2,1,0:T(4,128)(2,1)} %param.6) | data formatting | bytes 16384 | tf_op jit(solution)/shard_map/reshape | solution.py:378
  1.3 42.4 %shard_map.64 = bf16[16,256]{1,0:T(8,128)(2,1)} custom-call(bf16[16,256]{1,0:T(8,128)(2,1)} %reshape.15.vol, bf16[9,3,32,32]{3,2,1,0:T(8,128)(2,1)} %bitcast.4, bf16[9,3,32,32]{3,2,1,0:T(8,128)(2,1)} %bitcast.5, bf16[256,512]{1,0:T(8,128)(2,1)} %wl.1, bf16[9,3,16,512]{3,2,1,0:T(8,128)(2,1)} %bitcast.3, bf16[512,512]{1,0:T(8,128)(2,1)} %wu.1), custom_call_target="tpu_custom_call" | custom-call | tf_op jit(solution)/shard_map/pallas_call | solution.py:339
  43.7 1.3 %reshape.19 = bf16[4,4,256]{2,1,0:T(4,128)(2,1)} reshape(bf16[16,256]{1,0:T(8,128)(2,1)} %shard_map.64) | data formatting | bytes 16384 | tf_op jit(solution)/shard_map/reshape | solution.py:385

commit v3 on v2

v3 whole, which is shorter than its diff:
```python
import functools

import jax
import jax.numpy as jnp
from jax import lax
from jax.experimental import pallas as pl
from jax.experimental.pallas import tpu as pltpu
from jax.sharding import PartitionSpec as P

F32 = jnp.float32
BF16 = jnp.bfloat16
MESH = pl.DeviceIdType.MESH
BANDS = [(zi, zo) for zo in range(4) for zi in range(4) if abs(zi - zo) <= 1]
CHUNKS = [(0, 3), (3, 6), (6, 8), (8, 9)]
GAPS = [(zi, zo) for zo in range(4) for zi in range(4) if abs(zi - zo) > 1]


def gelu(v):
    return 0.5 * v * (1.0 + lax.erf(v * 0.7071067811865476))


def dot(a, b):
    return jnp.dot(a, b, preferred_element_type=F32)


def iota(shape, dim):
    return lax.broadcasted_iota(jnp.int32, shape, dim)


def one_hot(mask):
    return jnp.where(mask, 1.0, 0.0).astype(BF16)


def band_weights(w_ref, t_ref):
    spread = one_hot((iota((32, 256), 1) & 31) == iota((32, 256), 0))
    lane_z = iota((32, 256), 1) >> 5

    def body(tap, carry):
        w0 = dot(w_ref[tap, 0], spread)
        w1 = dot(w_ref[tap, 1], spread)
        w2 = dot(w_ref[tap, 2], spread)
        for zi in range(8):
            rows = jnp.where(
                lane_z == zi,
                w1,
                jnp.where(lane_z == zi - 1, w2, jnp.where(lane_z == zi + 1, w0, 0.0)),
            )
            t_ref[tap, zi * 32 : zi * 32 + 32, :] = rows.astype(BF16)
        return carry

    lax.fori_loop(0, 9, body, 0)


def kernel(
    groups, devices,
    vol, w1, w2, wl, wc, wu,
    out,
    blocks, w1_v, w2_v, wl_v, wu_v, t1, t2, raw, tc, wide, first, skip_p, send, recv, flat, cols, sums, parts, shares,
    load_sem, twin_sem, halo_s, halo_r, raw_s, raw_r, fwd_s, a2a_s, a2a_r, rs_s, rs_r,
):
    g = lax.axis_index("grp")
    d = lax.axis_index("dev")
    ring = devices // 4
    half = devices // 2
    lanes = wl.shape[1]
    width = lanes // 2
    tile = min(128, width)
    core = lax.rem(d, 2)
    zh = lax.rem(lax.div(d, 2), 2)
    ry = lax.div(d, 4)
    zl = lax.rem(g, 4)
    edge = (zl == 0) | (zl == 3)

    def member(dy, other_core):
        to_core = 1 - core if other_core else core
        return (lax.rem(ry + dy + ring, ring) * 2 + zh) * 2 + to_core

    def neighbour(dx, dy):
        return lax.rem(g + dx + groups, groups), lax.rem(d + dy + devices, devices)

    def across(to_core):
        return g + 3 - 2 * zl, (ry * 2 + 1 - zh) * 2 + to_core

    steps = [ring // 2]
    for k in range(ring // 2 - 1, 0, -1):
        steps += [k, -k]
    members = [(k, b) for k in steps for b in (0, 1)] + [(0, 1)]
    beside = [(dx, dy) for dx in (-1, 1) for dy in (-1, 1, 0)]
    outer = (g, lax.rem(d + 2 * core - 1 + devices, devices))

    barrier = pltpu.get_barrier_semaphore()
    partners = [outer] + [neighbour(*b) for b in beside] + [across(0), across(1)]
    partners += [(g, member(*m)) for m in members]
    for p in partners:
        pl.semaphore_signal(barrier, inc=1, device_id=p, device_id_type=MESH)

    mine = 2 * zh + core
    loads = [
        pltpu.make_async_copy(src, dst, load_sem.at[i])
        for i, (src, dst) in enumerate(
            [
                (vol, blocks.at[4]),
                (w1, w1_v),
                (w2, w2_v),
                (wl, wl_v),
                (wc.at[:, :, :, pl.ds(core * width, width)], raw.at[mine]),
                (wu, wu_v),
            ]
        )
    ]
    for c in loads:
        c.start()
    loads[0].wait()
    pl.semaphore_wait(barrier, len(partners))

    halo = []
    for dx, dy in [(0, -1), (0, 1)] + beside:
        slot = (1 - dx) * 3 + 1 - dy
        halo.append(
            pltpu.make_async_remote_copy(
                src_ref=blocks.at[4],
                dst_ref=blocks.at[slot],
                send_sem=halo_s.at[slot],
                recv_sem=halo_r.at[slot],
                device_id=neighbour(dx, dy),
                device_id_type=MESH,
            )
        )
        halo[-1].start()

    twin = pltpu.make_async_remote_copy(
        src_ref=wc.at[:, :, :, pl.ds((1 - core) * width, width)],
        dst_ref=raw.at[mine],
        send_sem=twin_sem.at[0],
        recv_sem=twin_sem.at[1],
        device_id=(g, member(0, 1)),
        device_id_type=MESH,
    )
    twin.start()

    def cross(i, to_core):
        lo, hi = CHUNKS[i]
        return pltpu.make_async_remote_copy(
            src_ref=wc.at[lo:hi, :, :, to_core * width : to_core * width + width],
            dst_ref=raw.at[mine, lo:hi],
            send_sem=raw_s.at[2 * i + to_core],
            recv_sem=raw_r.at[2 * i + core],
            device_id=across(to_core),
            device_id_type=MESH,
        )

    def inward(i, block):
        lo, hi = CHUNKS[i]
        there = 2 * (1 - zh) + block
        return pltpu.make_async_remote_copy(
            src_ref=raw.at[there, lo:hi],
            dst_ref=raw.at[there, lo:hi],
            send_sem=fwd_s.at[2 * i + block],
            recv_sem=raw_r.at[2 * i + block],
            device_id=(jnp.where(zl == 0, g + 1, g - 1), d),
            device_id_type=MESH,
        )

    @pl.when(edge)
    def _():
        for i in range(len(CHUNKS)):
            for to_core in range(2):
                cross(i, to_core).start()

    def pass_on(i):
        @pl.when(edge)
        def _():
            for block in range(2):
                inward(i, block).wait_recv()
                inward(i, block).start()

    def banded(block, lo, hi):
        for zi, zo in BANDS:
            tc[lo:hi, zi, block, :, zo * width : zo * width + width] = raw[block, lo:hi, zi - zo + 1]

    for zi, zo in GAPS:
        tc[:, zi, :, :, zo * width : zo * width + width] = jnp.zeros((9, 4, 16, width), BF16)
    wide[144:152] = jnp.zeros((8, 256), F32)
    first[120:128] = jnp.zeros((8, 256), F32)
    loads[1].wait()
    band_weights(w1_v, t1)
    loads[2].wait()
    band_weights(w2_v, t2)
    for c in loads[3:]:
        c.wait()
    banded(mine, 0, 9)

    row, col = iota((144, 144), 0), iota((144, 144), 1)
    slot = col >> 4
    sx = (slot >= 3).astype(jnp.int32) + (slot >= 6).astype(jnp.int32)
    sy = slot - 3 * sx
    fits = (sx * 4 + ((col >> 2) & 3)) * 12 + sy * 4 + (col & 3) == row
    gx, gy = g - 1 + sx, d - 1 + sy
    fits = fits & (gx >= 0) & (gx < groups) & (gy >= 0) & (gy < devices)
    place = one_hot(fits)

    pass_on(0)
    for c in halo:
        c.wait_recv()
    wide[0:144] = dot(place, blocks[...].reshape(144, 256))

    total = jnp.zeros((120, 256), F32)
    for tap in range(9):
        off = (tap // 3) * 12 + tap % 3
        total += dot(wide[off : off + 120].astype(BF16), t1[tap])
    rows = iota((120, 256), 0)
    rx = (rows * 171) >> 11
    fx, fy = 4 * g - 3 + rx, 4 * d - 3 + rows - 12 * rx
    inside = (fx >= 0) & (fx < 4 * groups) & (fy >= 0) & (fy < 4 * devices)
    act = gelu(total).astype(BF16).astype(F32)
    first[0:120] = jnp.where(inside, act, 0.0)

    total = jnp.zeros((96, 256), F32)
    for tap in range(9):
        off = (tap // 3) * 12 + tap % 3
        total += dot(first[off : off + 96].astype(BF16), t2[tap])
    skip = gelu(total).astype(BF16)

    row, col = iota((64, 96), 0), iota((64, 96), 1)
    ci, cj = (row >> 2) & 3, row & 3
    fits = (2 * ci + (row >> 5)) * 12 + 2 * cj + ((row >> 4) & 1) == col
    cx, cy = 2 * g - 1 + ci, 2 * d - 1 + cj
    fits = fits & (cx >= 0) & (cx < 2 * groups) & (cy >= 0) & (cy < 2 * devices)
    moved = dot(one_hot(fits), skip)
    skip_p[...] = moved
    stacked = jnp.concatenate(
        [
            jnp.concatenate(
                [moved[ab * 16 : ab * 16 + 16, k * 64 : k * 64 + 64] for ab in range(4)], axis=1
            )
            for k in range(4)
        ],
        axis=0,
    )
    lifted = gelu(dot(stacked.astype(BF16), wl_v[...]))
    for t in range(ring):
        send[t] = jnp.concatenate(
            [lifted[k * 16 : k * 16 + 16, t * 64 : t * 64 + 64] for k in range(4)], axis=1
        ).astype(BF16)

    me = 2 * ry + core

    def spread(m):
        to_y = lax.rem(ry + m[0] + ring, ring)
        to = 2 * to_y + (1 - core if m[1] else core)
        return pltpu.make_async_remote_copy(
            src_ref=send.at[to_y],
            dst_ref=recv.at[me],
            send_sem=a2a_s.at[to],
            recv_sem=a2a_r.at[me],
            device_id=(g, member(*m)),
            device_id_type=MESH,
        )

    for m in members:
        spread(m).start()
    recv[me] = send[ry]
    for i in range(1, len(CHUNKS)):
        pass_on(i)
    twin.wait_recv()
    banded(2 * zh + 1 - core, 0, 9)

    def arrive(off, carry):
        frm = lax.rem(me + off, half)
        pltpu.make_async_remote_copy(
            src_ref=send.at[0],
            dst_ref=recv.at[frm],
            send_sem=a2a_s.at[frm],
            recv_sem=a2a_r.at[frm],
            device_id=(g, d),
            device_id_type=MESH,
        ).wait_recv()
        return carry

    lax.fori_loop(1, half, arrive, 0)

    for lt in range(2):
        flat[lt] = recv[:, :, lt * 128 : lt * 128 + 128].astype(F32).reshape(16 * half, 128)
    for xx in range(4):
        for yb in range(4):
            for lt in range(2):
                piece = flat[lt, pl.ds(4 * xx + yb, half, stride=16), :].astype(BF16)
                for a in range(3):
                    for b in range(3):
                        ox, oy = xx - a, yb - b
                        if 0 <= ox < 2 and 0 <= oy < 2:
                            at, to = (2 * ox + oy) * half, (3 * a + b) * 256 + lt * 128
                            cols[at : at + half, to : to + 128] = piece

    @pl.when(jnp.logical_not(edge))
    def _():
        for i in range(len(CHUNKS)):
            for block in range(2):
                inward(i, block).wait_recv()

    for block in range(2):
        banded(2 * (1 - zh) + block, 0, 9)

    lhs = cols[...]
    for z in range(4):
        got = dot(lhs, tc[:, :, :, :, z * width : z * width + width].reshape(2304, width))
        for q in range(4):
            for lt in range(width // tile):
                sums[lt, pl.ds(4 * z + q, half, stride=16), :] = got[
                    q * half : q * half + half, lt * tile : lt * tile + tile
                ]
    for lt in range(width // tile):
        parts[:, :, lt * tile : lt * tile + tile] = sums[lt].reshape(half, 16, tile).astype(BF16)

    def share(m):
        to = 2 * lax.rem(ry + m[0] + ring, ring) + (1 - core if m[1] else core)
        return pltpu.make_async_remote_copy(
            src_ref=parts.at[to],
            dst_ref=shares.at[me],
            send_sem=rs_s.at[to],
            recv_sem=rs_r.at[me],
            device_id=(g, member(*m)),
            device_id_type=MESH,
        )

    for m in members:
        share(m).start()
    shares[me] = parts[me]

    def share_arrive(off, carry):
        frm = lax.rem(me + off, half)
        pltpu.make_async_remote_copy(
            src_ref=parts.at[0],
            dst_ref=shares.at[frm],
            send_sem=rs_s.at[frm],
            recv_sem=rs_r.at[frm],
            device_id=(g, d),
            device_id_type=MESH,
        ).wait_recv()
        return carry

    lax.fori_loop(1, half, share_arrive, 0)

    halves = []
    for h in range(2):
        total = shares[h].astype(F32)
        for t in range(1, ring):
            total += shares[2 * t + h].astype(F32)
        halves.append(total)
    coarse = gelu(jnp.concatenate(halves, axis=1)).astype(BF16)
    upper = dot(coarse, wu_v[...])

    def expand(base):
        return jnp.concatenate(
            [
                jnp.concatenate(
                    [
                        upper[4 * k : 4 * k + 4, base + ab * 64 : base + ab * 64 + 64]
                        for k in range(4)
                    ],
                    axis=1,
                )
                for ab in range(4)
            ],
            axis=0,
        )

    gate, value = expand(0), expand(256)
    own = jnp.concatenate(
        [skip_p[ab * 16 + 4 * i + 1 : ab * 16 + 4 * i + 3] for ab in range(4) for i in (1, 2)], axis=0
    )
    mixed = (own * jax.nn.sigmoid(gate) + value).astype(BF16)
    row, col = iota((16, 16), 0), iota((16, 16), 1)
    fits = ((row >> 2) == 2 * ((col >> 1) & 1) + (col >> 3)) & (
        (row & 3) == 2 * (col & 1) + ((col >> 2) & 1)
    )
    out[...] = dot(one_hot(fits), mixed).astype(BF16)

    for c in halo:
        c.wait_send()
    twin.wait_send()

    @pl.when(edge)
    def _():
        for i in range(len(CHUNKS)):
            for k in range(2):
                cross(i, k).wait_send()
                inward(i, k).wait_send()

    for m in members:
        spread(m).wait_send()
        share(m).wait_send()


def on_device(groups, devices, volume, w_first, w_second, w_lift, w_coarse, w_up):
    half = devices // 2
    wide = w_up.shape[0]
    tile = min(128, wide // 2)
    in_hbm = pl.BlockSpec(memory_space=pltpu.HBM)
    dma = pltpu.SemaphoreType.DMA
    result = pl.pallas_call(
        functools.partial(kernel, groups, devices),
        out_shape=jax.ShapeDtypeStruct((16, 256), BF16),
        in_specs=[pl.BlockSpec(memory_space=pl.ANY)] + [in_hbm] * 5,
        out_specs=pl.BlockSpec(memory_space=pltpu.VMEM),
        scratch_shapes=[
            pltpu.VMEM((9, 16, 256), BF16),
            pltpu.VMEM((9, 3, 32, 32), BF16),
            pltpu.VMEM((9, 3, 32, 32), BF16),
            pltpu.VMEM((256, wide), BF16),
            pltpu.VMEM((wide, 512), BF16),
            pltpu.VMEM((9, 256, 256), BF16),
            pltpu.VMEM((9, 256, 256), BF16),
            pltpu.VMEM((4, 9, 3, 16, wide // 2), BF16),
            pltpu.VMEM((9, 4, 4, 16, 2 * wide), BF16),
            pltpu.VMEM((152, 256), F32),
            pltpu.VMEM((128, 256), F32),
            pltpu.VMEM((64, 256), F32),
            pltpu.VMEM((devices // 4, 16, 256), BF16),
            pltpu.VMEM((half, 16, 256), BF16),
            pltpu.VMEM((2, 16 * half, 128), F32),
            pltpu.VMEM((4 * half, 2304), BF16),
            pltpu.VMEM((wide // 2 // tile, 16 * half, tile), F32),
            pltpu.VMEM((half, 16, wide // 2), BF16),
            pltpu.VMEM((half, 16, wide // 2), BF16),
            dma((6,)),
            dma((2,)),
            dma((9,)),
            dma((9,)),
            dma((2 * len(CHUNKS),)),
            dma((2 * len(CHUNKS),)),
            dma((2 * len(CHUNKS),)),
            dma((half,)),
            dma((half,)),
            dma((half,)),
            dma((half,)),
        ],
        compiler_params=pltpu.CompilerParams(
            collective_id=0, has_side_effects=True, vmem_limit_bytes=56 * 1024 * 1024
        ),
    )(
        volume.reshape(16, 256),
        w_first.reshape(9, 3, 32, 32),
        w_second.reshape(9, 3, 32, 32),
        w_lift,
        w_coarse.reshape(9, 3, 16, wide),
        w_up,
    )
    return result.reshape(4, 4, 256)


def solution(mesh):
    return jax.shard_map(
        functools.partial(on_device, mesh.shape["grp"], mesh.shape["dev"]),
        mesh=mesh,
        in_specs=(P("grp", "dev", None), P(), P(), P(), P(None, None, None, "dev", None), P()),
        out_specs=P("grp", "dev", None),
        check_vma=False,
    )
```

time: 45.3 us -> 41.1 us (0.907)
  the two profiles are of different devices: /device:TPU:1 before, /device:TPU:69 now
where the time goes in v3:
time: 41.1 us; the launch traced here: 40.9 us
  Pallas kernels  38.3 us (93%)
  local copies, waits for them, and re-layouts  2.61 us (6%)
    pallas_call x1, Pallas kernels, on_device(): pl.pallas_call(functools.partial(kernel, groups, devices), out_shape=jax....  38.3 us
    reshape x1, local copies, waits for them, and re-layouts, on_device(): return result.reshape(4, 4, 256)  1.3 us
    reshape x1, local copies, waits for them, and re-layouts, on_device(): volume.reshape(16, 256)  1.3 us

profile of v3, /device:TPU:69, one launch (start us, length us, event | category | flops | bytes accessed | tf_op | source)
XLA Modules:
  0.0 40.9 jit_solution(17667524434316500574)
XLA Ops:
  0.0 1.3 %reshape.15.vol = bf16[16,256]{1,0:T(8,128)(2,1)} reshape(bf16[4,4,256]{2,1,0:T(4,128)(2,1)} %param.6) | data formatting | bytes 16384 | tf_op jit(solution)/shard_map/reshape | solution.py:442
  1.3 38.3 %shard_map.64 = bf16[16,256]{1,0:T(8,128)(2,1)} custom-call(bf16[16,256]{1,0:T(8,128)(2,1)} %reshape.15.vol, bf16[9,3,32,32]{3,2,1,0:T(8,128)(2,1)} %bitcast.4, bf16[9,3,32,32]{3,2,1,0:T(8,128)(2,1)} %bitcast.5, bf16[256,512]{1,0:T(8,128)(2,1)} %wl.1, bf16[9,3,16,512]{3,2,1,0:T(8,128)(2,1)} %bitcast.3, bf16[512,512]{1,0:T(8,128)(2,1)} %wu.1), custom_call_target="tpu_custom_call" | custom-call | tf_op jit(solution)/shard_map/pallas_call | solution.py:401
  39.6 1.3 %reshape.19 = bf16[4,4,256]{2,1,0:T(4,128)(2,1)} reshape(bf16[16,256]{1,0:T(8,128)(2,1)} %shard_map.64) | data formatting | bytes 16384 | tf_op jit(solution)/shard_map/reshape | solution.py:449

commit v4 on v3

--- a/solution.py
+++ b/solution.py
@@ -55,8 +55,8 @@
     groups, devices,
     vol, w1, w2, wl, wc, wu,
     out,
-    blocks, w1_v, w2_v, wl_v, wu_v, t1, t2, raw, tc, wide, first, skip_p, send, recv, flat, cols, sums, parts, shares,
-    load_sem, twin_sem, halo_s, halo_r, raw_s, raw_r, fwd_s, a2a_s, a2a_r, rs_s, rs_r,
+    block_v, blocks, w1_v, w2_v, wl_v, wu_v, t1, t2, raw, tc, wide, first, skip_p, send, recv, flat, cols, sums, parts, shares,
+    load_sem, twin_sem, halo_s, halo_r, raw_s, raw_r, fwd_s, side_s, side_r, a2a_s, a2a_r, rs_s, rs_r,
 ):
     g = lax.axis_index("grp")
     d = lax.axis_index("dev")
@@ -81,6 +81,9 @@
     def across(to_core):
         return g + 3 - 2 * zl, (ry * 2 + 1 - zh) * 2 + to_core
 
+    xp = lax.rem(lax.div(g, 4), 2)
+    aside = (g + 4 - 8 * xp, d)
+
     steps = [ring // 2]
     for k in range(ring // 2 - 1, 0, -1):
         steps += [k, -k]
@@ -90,7 +93,7 @@
 
     barrier = pltpu.get_barrier_semaphore()
     partners = [outer] + [neighbour(*b) for b in beside] + [across(0), across(1)]
-    partners += [(g, member(*m)) for m in members]
+    partners += [aside] + [(g, member(*m)) for m in members]
     for p in partners:
         pl.semaphore_signal(barrier, inc=1, device_id=p, device_id_type=MESH)
 
@@ -99,7 +102,7 @@
         pltpu.make_async_copy(src, dst, load_sem.at[i])
         for i, (src, dst) in enumerate(
             [
-                (vol, blocks.at[4]),
+                (vol, block_v),
                 (w1, w1_v),
                 (w2, w2_v),
                 (wl, wl_v),
@@ -111,6 +114,7 @@
     for c in loads:
         c.start()
     loads[0].wait()
+    blocks[4] = block_v[...].astype(F32).reshape(16, 256).astype(BF16)
     pl.semaphore_wait(barrier, len(partners))
 
     halo = []
@@ -138,26 +142,29 @@
     )
     twin.start()
 
+    part = width // 2
+
     def cross(i, to_core):
         lo, hi = CHUNKS[i]
         return pltpu.make_async_remote_copy(
-            src_ref=wc.at[lo:hi, :, :, to_core * width : to_core * width + width],
-            dst_ref=raw.at[mine, lo:hi],
+            src_ref=wc.at[lo:hi, :, :, pl.ds(to_core * width + xp * part, part)],
+            dst_ref=raw.at[mine, lo:hi, :, :, pl.ds(xp * part, part)],
             send_sem=raw_s.at[2 * i + to_core],
             recv_sem=raw_r.at[2 * i + core],
             device_id=across(to_core),
             device_id_type=MESH,
         )
 
-    def inward(i, block):
+    def onward(i, block, sideways):
         lo, hi = CHUNKS[i]
         there = 2 * (1 - zh) + block
+        here = raw.at[there, lo:hi, :, :, pl.ds(xp * part, part)]
         return pltpu.make_async_remote_copy(
-            src_ref=raw.at[there, lo:hi],
-            dst_ref=raw.at[there, lo:hi],
-            send_sem=fwd_s.at[2 * i + block],
-            recv_sem=raw_r.at[2 * i + block],
-            device_id=(jnp.where(zl == 0, g + 1, g - 1), d),
+            src_ref=here,
+            dst_ref=here,
+            send_sem=(side_s if sideways else fwd_s).at[2 * i + block],
+            recv_sem=(side_r if sideways else raw_r).at[2 * i + block],
+            device_id=aside if sideways else (jnp.where(zl == 0, g + 1, g - 1), d),
             device_id_type=MESH,
         )
 
@@ -167,12 +174,15 @@
             for to_core in range(2):
                 cross(i, to_core).start()
 
-    def pass_on(i):
-        @pl.when(edge)
+    def pass_on(where, chunks):
+        @pl.when(edge if where else jnp.logical_not(edge))
         def _():
-            for block in range(2):
-                inward(i, block).wait_recv()
-                inward(i, block).start()
+            for i in chunks:
+                for block in range(2):
+                    onward(i, block, False).wait_recv()
+                    if where:
+                        onward(i, block, False).start()
+                    onward(i, block, True).start()
 
     def banded(block, lo, hi):
         for zi, zo in BANDS:
@@ -199,7 +209,7 @@
     fits = fits & (gx >= 0) & (gx < groups) & (gy >= 0) & (gy < devices)
     place = one_hot(fits)
 
-    pass_on(0)
+    pass_on(True, [0])
     for c in halo:
         c.wait_recv()
     wide[0:144] = dot(place, blocks[...].reshape(144, 256))
@@ -214,6 +224,8 @@
     inside = (fx >= 0) & (fx < 4 * groups) & (fy >= 0) & (fy < 4 * devices)
     act = gelu(total).astype(BF16).astype(F32)
     first[0:120] = jnp.where(inside, act, 0.0)
+
+    pass_on(True, [1])
 
     total = jnp.zeros((96, 256), F32)
     for tap in range(9):
@@ -260,8 +272,8 @@
     for m in members:
         spread(m).start()
     recv[me] = send[ry]
-    for i in range(1, len(CHUNKS)):
-        pass_on(i)
+    pass_on(True, range(2, len(CHUNKS)))
+    pass_on(False, range(len(CHUNKS)))
     twin.wait_recv()
     banded(2 * zh + 1 - core, 0, 9)
 
@@ -292,12 +304,18 @@
                             at, to = (2 * ox + oy) * half, (3 * a + b) * 256 + lt * 128
                             cols[at : at + half, to : to + 128] = piece
 
-    @pl.when(jnp.logical_not(edge))
-    def _():
-        for i in range(len(CHUNKS)):
-            for block in range(2):
-                inward(i, block).wait_recv()
-
+    for i in range(len(CHUNKS)):
+        for block in range(2):
+            lo, hi = CHUNKS[i]
+            there = raw.at[2 * (1 - zh) + block, lo:hi, :, :, pl.ds((1 - xp) * part, part)]
+            pltpu.make_async_remote_copy(
+                src_ref=there,
+                dst_ref=there,
+                send_sem=side_s.at[2 * i + block],
+                recv_sem=side_r.at[2 * i + block],
+                device_id=aside,
+                device_id_type=MESH,
+            ).wait_recv()
     for block in range(2):
         banded(2 * (1 - zh) + block, 0, 9)
 
@@ -374,7 +392,7 @@
     fits = ((row >> 2) == 2 * ((col >> 1) & 1) + (col >> 3)) & (
         (row & 3) == 2 * (col & 1) + ((col >> 2) & 1)
     )
-    out[...] = dot(one_hot(fits), mixed).astype(BF16)
+    out[...] = dot(one_hot(fits), mixed).reshape(4, 4, 256).astype(BF16)
 
     for c in halo:
         c.wait_send()
@@ -385,7 +403,11 @@
         for i in range(len(CHUNKS)):
             for k in range(2):
                 cross(i, k).wait_send()
-                inward(i, k).wait_send()
+                onward(i, k, False).wait_send()
+
+    for i in range(len(CHUNKS)):
+        for k in range(2):
+            onward(i, k, True).wait_send()
 
     for m in members:
         spread(m).wait_send()
@@ -400,10 +422,11 @@
     dma = pltpu.SemaphoreType.DMA
     result = pl.pallas_call(
         functools.partial(kernel, groups, devices),
-        out_shape=jax.ShapeDtypeStruct((16, 256), BF16),
+        out_shape=jax.ShapeDtypeStruct((4, 4, 256), BF16),
         in_specs=[pl.BlockSpec(memory_space=pl.ANY)] + [in_hbm] * 5,
         out_specs=pl.BlockSpec(memory_space=pltpu.VMEM),
         scratch_shapes=[
+            pltpu.VMEM((4, 4, 256), BF16),
             pltpu.VMEM((9, 16, 256), BF16),
             pltpu.VMEM((9, 3, 32, 32), BF16),
             pltpu.VMEM((9, 3, 32, 32), BF16),
@@ -430,6 +453,8 @@
             dma((2 * len(CHUNKS),)),
             dma((2 * len(CHUNKS),)),
             dma((2 * len(CHUNKS),)),
+            dma((2 * len(CHUNKS),)),
+            dma((2 * len(CHUNKS),)),
             dma((half,)),
             dma((half,)),
             dma((half,)),
@@ -439,14 +464,14 @@
             collective_id=0, has_side_effects=True, vmem_limit_bytes=56 * 1024 * 1024
         ),
     )(
-        volume.reshape(16, 256),
+        volume,
         w_first.reshape(9, 3, 32, 32),
         w_second.reshape(9, 3, 32, 32),
         w_lift,
         w_coarse.reshape(9, 3, 16, wide),
         w_up,
     )
-    return result.reshape(4, 4, 256)
+    return result
 
 
 def solution(mesh):

time: 41.1 us -> 38.8 us (0.944)
  the two profiles are of different devices: /device:TPU:69 before, /device:TPU:1 now
where the time goes in v4:
time: 38.8 us; the launch traced here: 38.6 us
  Pallas kernels  37.3 us (96%)
  local copies, waits for them, and re-layouts  1.3 us (3%)
    pallas_call x1, Pallas kernels, on_device(): pl.pallas_call(functools.partial(kernel, groups, devices), out_shape=jax....  37.3 us
    unnamed x1, local copies, waits for them, and re-layouts  1.3 us

profile of v4, /device:TPU:1, one launch (start us, length us, event | category | flops | bytes accessed | tf_op | source)
XLA Modules:
  0.0 38.6 jit_solution(14002576013352613883)
XLA Ops:
  0.0 37.3 %shard_map.64 = bf16[4,4,256]{2,1,0:T(4,128)(2,1)} custom-call(bf16[4,4,256]{2,1,0:T(4,128)(2,1)} %vol.1, bf16[9,3,32,32]{3,2,1,0:T(8,128)(2,1)} %bitcast.4, bf16[9,3,32,32]{3,2,1,0:T(8,128)(2,1)} %bitcast.5, bf16[256,512]{1,0:T(8,128)(2,1)} %wl.1, bf16[9,3,16,512]{3,2,1,0:T(8,128)(2,1)} %bitcast.3, bf16[512,512]{1,0:T(8,128)(2,1)} %wu.1), custom_call_target="tpu_custom_call" | custom-call | tf_op jit(solution)/shard_map/pallas_call | solution.py:423
  37.3 1.3 %copy.8 = bf16[4,4,256]{2,1,0:T(4,128)(2,1)} copy(bf16[4,4,256]{2,1,0:T(4,128)(2,1)} %shard_map.64) | data formatting | bytes 16384

commit v5 on v4

--- a/solution.py
+++ b/solution.py
@@ -11,7 +11,7 @@
 BF16 = jnp.bfloat16
 MESH = pl.DeviceIdType.MESH
 BANDS = [(zi, zo) for zo in range(4) for zi in range(4) if abs(zi - zo) <= 1]
-CHUNKS = [(0, 3), (3, 6), (6, 8), (8, 9)]
+CHUNKS = [(0, 4), (4, 7), (7, 9)]
 GAPS = [(zi, zo) for zo in range(4) for zi in range(4) if abs(zi - zo) > 1]
 
 
@@ -56,7 +56,7 @@
     vol, w1, w2, wl, wc, wu,
     out,
     block_v, blocks, w1_v, w2_v, wl_v, wu_v, t1, t2, raw, tc, wide, first, skip_p, send, recv, flat, cols, sums, parts, shares,
-    load_sem, twin_sem, halo_s, halo_r, raw_s, raw_r, fwd_s, side_s, side_r, a2a_s, a2a_r, rs_s, rs_r,
+    load_sem, twin_sem, halo_s, halo_r, raw_s, raw_r, fwd_s, fwd_r, side_s, side_r, a2a_s, a2a_r, rs_s, rs_r,
 ):
     g = lax.axis_index("grp")
     d = lax.axis_index("dev")
@@ -89,20 +89,38 @@
         steps += [k, -k]
     members = [(k, b) for k in steps for b in (0, 1)] + [(0, 1)]
     beside = [(dx, dy) for dx in (-1, 1) for dy in (-1, 1, 0)]
-    outer = (g, lax.rem(d + 2 * core - 1 + devices, devices))
+    around = [(0, -1), (0, 1)] + beside
+
+    def exists(dx, dy):
+        there = (d + dy >= 0) & (d + dy < devices)
+        return there & (g + dx >= 0) & (g + dx < groups)
 
     barrier = pltpu.get_barrier_semaphore()
-    partners = [outer] + [neighbour(*b) for b in beside] + [across(0), across(1)]
-    partners += [aside] + [(g, member(*m)) for m in members]
+    first_load = pltpu.make_async_copy(vol, block_v, load_sem.at[0])
+    first_load.start()
+    sibling = 1 - 2 * core
+    greeted = 0
+    for dx, dy in around:
+        wanted = exists(dx, dy)
+        if dx == 0:
+            wanted = wanted & (sibling != dy)
+        greeted += wanted.astype(jnp.int32)
+
+        @pl.when(wanted)
+        def _():
+            pl.semaphore_signal(
+                barrier, inc=1, device_id=neighbour(dx, dy), device_id_type=MESH
+            )
+
+    partners = [across(0), across(1), aside] + [(g, member(*m)) for m in members]
     for p in partners:
         pl.semaphore_signal(barrier, inc=1, device_id=p, device_id_type=MESH)
 
     mine = 2 * zh + core
     loads = [
-        pltpu.make_async_copy(src, dst, load_sem.at[i])
+        pltpu.make_async_copy(src, dst, load_sem.at[i + 1])
         for i, (src, dst) in enumerate(
             [
-                (vol, block_v),
                 (w1, w1_v),
                 (w2, w2_v),
                 (wl, wl_v),
@@ -113,24 +131,25 @@
     ]
     for c in loads:
         c.start()
-    loads[0].wait()
+    first_load.wait()
     blocks[4] = block_v[...].astype(F32).reshape(16, 256).astype(BF16)
-    pl.semaphore_wait(barrier, len(partners))
-
-    halo = []
-    for dx, dy in [(0, -1), (0, 1)] + beside:
-        slot = (1 - dx) * 3 + 1 - dy
-        halo.append(
-            pltpu.make_async_remote_copy(
-                src_ref=blocks.at[4],
-                dst_ref=blocks.at[slot],
-                send_sem=halo_s.at[slot],
-                recv_sem=halo_r.at[slot],
-                device_id=neighbour(dx, dy),
-                device_id_type=MESH,
-            )
-        )
-        halo[-1].start()
+    pl.semaphore_wait(barrier, greeted + len(partners))
+
+    def block_copy(dx, dy, slot):
+        return pltpu.make_async_remote_copy(
+            src_ref=blocks.at[4],
+            dst_ref=blocks.at[slot],
+            send_sem=halo_s.at[slot],
+            recv_sem=halo_r.at[slot],
+            device_id=neighbour(dx, dy),
+            device_id_type=MESH,
+        )
+
+    for dx, dy in around:
+
+        @pl.when(exists(dx, dy))
+        def _():
+            block_copy(dx, dy, (1 - dx) * 3 + 1 - dy).start()
 
     twin = pltpu.make_async_remote_copy(
         src_ref=wc.at[:, :, :, pl.ds((1 - core) * width, width)],
@@ -155,15 +174,16 @@
             device_id_type=MESH,
         )
 
-    def onward(i, block, sideways):
+    foreign = 2 * (1 - zh)
+
+    def onward(i, sideways):
         lo, hi = CHUNKS[i]
-        there = 2 * (1 - zh) + block
-        here = raw.at[there, lo:hi, :, :, pl.ds(xp * part, part)]
+        here = raw.at[pl.ds(foreign, 2), lo:hi, :, :, pl.ds(xp * part, part)]
         return pltpu.make_async_remote_copy(
             src_ref=here,
             dst_ref=here,
-            send_sem=(side_s if sideways else fwd_s).at[2 * i + block],
-            recv_sem=(side_r if sideways else raw_r).at[2 * i + block],
+            send_sem=(side_s if sideways else fwd_s).at[i],
+            recv_sem=(side_r if sideways else fwd_r).at[i],
             device_id=aside if sideways else (jnp.where(zl == 0, g + 1, g - 1), d),
             device_id_type=MESH,
         )
@@ -174,15 +194,29 @@
             for to_core in range(2):
                 cross(i, to_core).start()
 
+    def crossed(i, block):
+        lo, hi = CHUNKS[i]
+        there = raw.at[foreign + block, lo:hi, :, :, pl.ds(xp * part, part)]
+        return pltpu.make_async_remote_copy(
+            src_ref=there,
+            dst_ref=there,
+            send_sem=raw_s.at[2 * i + block],
+            recv_sem=raw_r.at[2 * i + block],
+            device_id=across(block),
+            device_id_type=MESH,
+        )
+
     def pass_on(where, chunks):
         @pl.when(edge if where else jnp.logical_not(edge))
         def _():
             for i in chunks:
-                for block in range(2):
-                    onward(i, block, False).wait_recv()
-                    if where:
-                        onward(i, block, False).start()
-                    onward(i, block, True).start()
+                if where:
+                    crossed(i, 0).wait_recv()
+                    crossed(i, 1).wait_recv()
+                    onward(i, False).start()
+                else:
+                    onward(i, False).wait_recv()
+                onward(i, True).start()
 
     def banded(block, lo, hi):
         for zi, zo in BANDS:
@@ -192,11 +226,11 @@
         tc[:, zi, :, :, zo * width : zo * width + width] = jnp.zeros((9, 4, 16, width), BF16)
     wide[144:152] = jnp.zeros((8, 256), F32)
     first[120:128] = jnp.zeros((8, 256), F32)
+    loads[0].wait()
+    band_weights(w1_v, t1)
     loads[1].wait()
-    band_weights(w1_v, t1)
-    loads[2].wait()
     band_weights(w2_v, t2)
-    for c in loads[3:]:
+    for c in loads[2:]:
         c.wait()
     banded(mine, 0, 9)
 
@@ -210,8 +244,17 @@
     place = one_hot(fits)
 
     pass_on(True, [0])
-    for c in halo:
-        c.wait_recv()
+    for dx, dy in around:
+        slot = (1 + dx) * 3 + 1 + dy
+
+        @pl.when(exists(dx, dy))
+        def _():
+            block_copy(dx, dy, slot).wait_recv()
+
+        @pl.when(jnp.logical_not(exists(dx, dy)))
+        def _():
+            blocks[slot] = jnp.zeros((16, 256), BF16)
+
     wide[0:144] = dot(place, blocks[...].reshape(144, 256))
 
     total = jnp.zeros((120, 256), F32)
@@ -305,19 +348,18 @@
                             cols[at : at + half, to : to + 128] = piece
 
     for i in range(len(CHUNKS)):
-        for block in range(2):
-            lo, hi = CHUNKS[i]
-            there = raw.at[2 * (1 - zh) + block, lo:hi, :, :, pl.ds((1 - xp) * part, part)]
-            pltpu.make_async_remote_copy(
-                src_ref=there,
-                dst_ref=there,
-                send_sem=side_s.at[2 * i + block],
-                recv_sem=side_r.at[2 * i + block],
-                device_id=aside,
-                device_id_type=MESH,
-            ).wait_recv()
+        lo, hi = CHUNKS[i]
+        there = raw.at[pl.ds(foreign, 2), lo:hi, :, :, pl.ds((1 - xp) * part, part)]
+        pltpu.make_async_remote_copy(
+            src_ref=there,
+            dst_ref=there,
+            send_sem=side_s.at[i],
+            recv_sem=side_r.at[i],
+            device_id=aside,
+            device_id_type=MESH,
+        ).wait_recv()
     for block in range(2):
-        banded(2 * (1 - zh) + block, 0, 9)
+        banded(foreign + block, 0, 9)
 
     lhs = cols[...]
     for z in range(4):
@@ -394,8 +436,12 @@
     )
     out[...] = dot(one_hot(fits), mixed).reshape(4, 4, 256).astype(BF16)
 
-    for c in halo:
-        c.wait_send()
+    for dx, dy in around:
+
+        @pl.when(exists(dx, dy))
+        def _():
+            block_copy(dx, dy, (1 - dx) * 3 + 1 - dy).wait_send()
+
     twin.wait_send()
 
     @pl.when(edge)
@@ -403,11 +449,10 @@
         for i in range(len(CHUNKS)):
             for k in range(2):
                 cross(i, k).wait_send()
-                onward(i, k, False).wait_send()
+            onward(i, False).wait_send()
 
     for i in range(len(CHUNKS)):
-        for k in range(2):
-            onward(i, k, True).wait_send()
+        onward(i, True).wait_send()
 
     for m in members:
         spread(m).wait_send()
@@ -452,9 +497,10 @@
             dma((9,)),
             dma((2 * len(CHUNKS),)),
             dma((2 * len(CHUNKS),)),
-            dma((2 * len(CHUNKS),)),
-            dma((2 * len(CHUNKS),)),
-            dma((2 * len(CHUNKS),)),
+            dma((len(CHUNKS),)),
+            dma((len(CHUNKS),)),
+            dma((len(CHUNKS),)),
+            dma((len(CHUNKS),)),
             dma((half,)),
             dma((half,)),
             dma((half,)),

time: 38.8 us -> 39.5 us (1.018)
  the two profiles are of different devices: /device:TPU:1 before, /device:TPU:65 now
where the time goes in v5:
time: 39.5 us; the launch traced here: 39.3 us
  Pallas kernels  38 us (96%)
  local copies, waits for them, and re-layouts  1.3 us (3%)
    pallas_call x1, Pallas kernels, on_device(): pl.pallas_call(functools.partial(kernel, groups, devices), out_shape=jax....  38 us
    unnamed x1, local copies, waits for them, and re-layouts  1.3 us

profile of v5, /device:TPU:65, one launch (start us, length us, event | category | flops | bytes accessed | tf_op | source)
XLA Modules:
  0.0 39.3 jit_solution(14056635809925284489)
XLA Ops:
  0.0 38.0 %shard_map.64 = bf16[4,4,256]{2,1,0:T(4,128)(2,1)} custom-call(bf16[4,4,256]{2,1,0:T(4,128)(2,1)} %vol.1, bf16[9,3,32,32]{3,2,1,0:T(8,128)(2,1)} %bitcast.4, bf16[9,3,32,32]{3,2,1,0:T(8,128)(2,1)} %bitcast.5, bf16[256,512]{1,0:T(8,128)(2,1)} %wl.1, bf16[9,3,16,512]{3,2,1,0:T(8,128)(2,1)} %bitcast.3, bf16[512,512]{1,0:T(8,128)(2,1)} %wu.1), custom_call_target="tpu_custom_call" | custom-call | tf_op jit(solution)/shard_map/pallas_call | solution.py:468
  38.0 1.3 %copy.8 = bf16[4,4,256]{2,1,0:T(4,128)(2,1)} copy(bf16[4,4,256]{2,1,0:T(4,128)(2,1)} %shard_map.64) | data formatting | bytes 16384

commit v6 on v5

--- a/solution.py
+++ b/solution.py
@@ -55,7 +55,7 @@
     groups, devices,
     vol, w1, w2, wl, wc, wu,
     out,
-    block_v, blocks, w1_v, w2_v, wl_v, wu_v, t1, t2, raw, tc, wide, first, skip_p, send, recv, flat, cols, sums, parts, shares,
+    block_v, blocks, w1_v, w2_v, wl_v, wu_v, t1, t2, wq, raw, tc, wide, first, skip_p, send, recv, flat, cols, sums, parts, shares,
     load_sem, twin_sem, halo_s, halo_r, raw_s, raw_r, fwd_s, fwd_r, side_s, side_r, a2a_s, a2a_r, rs_s, rs_r,
 ):
     g = lax.axis_index("grp")
@@ -64,6 +64,7 @@
     half = devices // 2
     lanes = wl.shape[1]
     width = lanes // 2
+    part = width // 2
     tile = min(128, width)
     core = lax.rem(d, 2)
     zh = lax.rem(lax.div(d, 2), 2)
@@ -124,12 +125,17 @@
                 (w1, w1_v),
                 (w2, w2_v),
                 (wl, wl_v),
-                (wc.at[:, :, :, pl.ds(core * width, width)], raw.at[mine]),
                 (wu, wu_v),
             ]
         )
     ]
-    for c in loads:
+    quarters = [
+        pltpu.make_async_copy(
+            wc.at[:, :, :, q * part : q * part + part], wq.at[q], load_sem.at[5 + q]
+        )
+        for q in range(4)
+    ]
+    for c in quarters + loads:
         c.start()
     first_load.wait()
     blocks[4] = block_v[...].astype(F32).reshape(16, 256).astype(BF16)
@@ -151,8 +157,10 @@
         def _():
             block_copy(dx, dy, (1 - dx) * 3 + 1 - dy).start()
 
+    for c in quarters:
+        c.wait()
     twin = pltpu.make_async_remote_copy(
-        src_ref=wc.at[:, :, :, pl.ds((1 - core) * width, width)],
+        src_ref=wq.at[pl.ds(2 - 2 * core, 2)],
         dst_ref=raw.at[mine],
         send_sem=twin_sem.at[0],
         recv_sem=twin_sem.at[1],
@@ -161,13 +169,11 @@
     )
     twin.start()
 
-    part = width // 2
-
     def cross(i, to_core):
         lo, hi = CHUNKS[i]
         return pltpu.make_async_remote_copy(
-            src_ref=wc.at[lo:hi, :, :, pl.ds(to_core * width + xp * part, part)],
-            dst_ref=raw.at[mine, lo:hi, :, :, pl.ds(xp * part, part)],
+            src_ref=wq.at[2 * to_core + xp, lo:hi],
+            dst_ref=raw.at[mine, xp, lo:hi],
             send_sem=raw_s.at[2 * i + to_core],
             recv_sem=raw_r.at[2 * i + core],
             device_id=across(to_core),
@@ -178,7 +184,7 @@
 
     def onward(i, sideways):
         lo, hi = CHUNKS[i]
-        here = raw.at[pl.ds(foreign, 2), lo:hi, :, :, pl.ds(xp * part, part)]
+        here = raw.at[pl.ds(foreign, 2), xp, lo:hi]
         return pltpu.make_async_remote_copy(
             src_ref=here,
             dst_ref=here,
@@ -196,7 +202,7 @@
 
     def crossed(i, block):
         lo, hi = CHUNKS[i]
-        there = raw.at[foreign + block, lo:hi, :, :, pl.ds(xp * part, part)]
+        there = raw.at[foreign + block, xp, lo:hi]
         return pltpu.make_async_remote_copy(
             src_ref=there,
             dst_ref=there,
@@ -218,9 +224,11 @@
                     onward(i, False).wait_recv()
                 onward(i, True).start()
 
-    def banded(block, lo, hi):
-        for zi, zo in BANDS:
-            tc[lo:hi, zi, block, :, zo * width : zo * width + width] = raw[block, lo:hi, zi - zo + 1]
+    def banded(block, source):
+        for h in range(2):
+            for zi, zo in BANDS:
+                at = zo * width + h * part
+                tc[:, zi, block, :, at : at + part] = source[h][:, zi - zo + 1]
 
     for zi, zo in GAPS:
         tc[:, zi, :, :, zo * width : zo * width + width] = jnp.zeros((9, 4, 16, width), BF16)
@@ -232,7 +240,7 @@
     band_weights(w2_v, t2)
     for c in loads[2:]:
         c.wait()
-    banded(mine, 0, 9)
+    banded(mine, [wq.at[2 * core + h] for h in range(2)])
 
     row, col = iota((144, 144), 0), iota((144, 144), 1)
     slot = col >> 4
@@ -318,7 +326,7 @@
     pass_on(True, range(2, len(CHUNKS)))
     pass_on(False, range(len(CHUNKS)))
     twin.wait_recv()
-    banded(2 * zh + 1 - core, 0, 9)
+    banded(2 * zh + 1 - core, [raw.at[2 * zh + 1 - core, h] for h in range(2)])
 
     def arrive(off, carry):
         frm = lax.rem(me + off, half)
@@ -349,7 +357,7 @@
 
     for i in range(len(CHUNKS)):
         lo, hi = CHUNKS[i]
-        there = raw.at[pl.ds(foreign, 2), lo:hi, :, :, pl.ds((1 - xp) * part, part)]
+        there = raw.at[pl.ds(foreign, 2), 1 - xp, lo:hi]
         pltpu.make_async_remote_copy(
             src_ref=there,
             dst_ref=there,
@@ -359,7 +367,7 @@
             device_id_type=MESH,
         ).wait_recv()
     for block in range(2):
-        banded(foreign + block, 0, 9)
+        banded(foreign + block, [raw.at[foreign + block, h] for h in range(2)])
 
     lhs = cols[...]
     for z in range(4):
@@ -479,7 +487,8 @@
             pltpu.VMEM((wide, 512), BF16),
             pltpu.VMEM((9, 256, 256), BF16),
             pltpu.VMEM((9, 256, 256), BF16),
-            pltpu.VMEM((4, 9, 3, 16, wide // 2), BF16),
+            pltpu.VMEM((4, 9, 3, 16, wide // 4), BF16),
+            pltpu.VMEM((4, 2, 9, 3, 16, wide // 4), BF16),
             pltpu.VMEM((9, 4, 4, 16, 2 * wide), BF16),
             pltpu.VMEM((152, 256), F32),
             pltpu.VMEM((128, 256), F32),
@@ -491,7 +500,7 @@
             pltpu.VMEM((wide // 2 // tile, 16 * half, tile), F32),
             pltpu.VMEM((half, 16, wide // 2), BF16),
             pltpu.VMEM((half, 16, wide // 2), BF16),
-            dma((6,)),
+            dma((9,)),
             dma((2,)),
             dma((9,)),
             dma((9,)),

time: 39.5 us -> 39.4 us (level)
  the two profiles are of different devices: /device:TPU:65 before, /device:TPU:1 now
where the time goes in v6:
time: 39.4 us; the launch traced here: 39 us
  Pallas kernels  37.7 us (96%)
  local copies, waits for them, and re-layouts  1.3 us (3%)
    pallas_call x1, Pallas kernels, on_device(): pl.pallas_call(functools.partial(kernel, groups, devices), out_shape=jax....  37.7 us
    unnamed x1, local copies, waits for them, and re-layouts  1.3 us

profile of v6, /device:TPU:1, one launch (start us, length us, event | category | flops | bytes accessed | tf_op | source)
XLA Modules:
  0.0 39.0 jit_solution(11962668124872669759)
XLA Ops:
  0.0 37.7 %shard_map.64 = bf16[4,4,256]{2,1,0:T(4,128)(2,1)} custom-call(bf16[4,4,256]{2,1,0:T(4,128)(2,1)} %vol.1, bf16[9,3,32,32]{3,2,1,0:T(8,128)(2,1)} %bitcast.4, bf16[9,3,32,32]{3,2,1,0:T(8,128)(2,1)} %bitcast.5, bf16[256,512]{1,0:T(8,128)(2,1)} %wl.1, bf16[9,3,16,512]{3,2,1,0:T(8,128)(2,1)} %bitcast.3, bf16[512,512]{1,0:T(8,128)(2,1)} %wu.1), custom_call_target="tpu_custom_call" | custom-call | tf_op jit(solution)/shard_map/pallas_call | solution.py:476
  37.7 1.3 %copy.8 = bf16[4,4,256]{2,1,0:T(4,128)(2,1)} copy(bf16[4,4,256]{2,1,0:T(4,128)(2,1)} %shard_map.64) | data formatting | bytes 16384

commit v7 on v6

--- a/solution.py
+++ b/solution.py
@@ -212,10 +212,10 @@
             device_id_type=MESH,
         )
 
-    def pass_on(where, chunks):
+    def pass_on(where):
         @pl.when(edge if where else jnp.logical_not(edge))
         def _():
-            for i in chunks:
+            for i in range(len(CHUNKS)):
                 if where:
                     crossed(i, 0).wait_recv()
                     crossed(i, 1).wait_recv()
@@ -251,7 +251,6 @@
     fits = fits & (gx >= 0) & (gx < groups) & (gy >= 0) & (gy < devices)
     place = one_hot(fits)
 
-    pass_on(True, [0])
     for dx, dy in around:
         slot = (1 + dx) * 3 + 1 + dy
 
@@ -275,8 +274,6 @@
     inside = (fx >= 0) & (fx < 4 * groups) & (fy >= 0) & (fy < 4 * devices)
     act = gelu(total).astype(BF16).astype(F32)
     first[0:120] = jnp.where(inside, act, 0.0)
-
-    pass_on(True, [1])
 
     total = jnp.zeros((96, 256), F32)
     for tap in range(9):
@@ -323,10 +320,10 @@
     for m in members:
         spread(m).start()
     recv[me] = send[ry]
-    pass_on(True, range(2, len(CHUNKS)))
-    pass_on(False, range(len(CHUNKS)))
     twin.wait_recv()
     banded(2 * zh + 1 - core, [raw.at[2 * zh + 1 - core, h] for h in range(2)])
+    pass_on(True)
+    pass_on(False)
 
     def arrive(off, carry):
         frm = lax.rem(me + off, half)

time: 39.4 us -> 39.1 us (level)
  the two profiles are of different devices: /device:TPU:1 before, /device:TPU:65 now
where the time goes in v7:
time: 39.1 us; the launch traced here: 38.9 us
  Pallas kernels  37.6 us (96%)
  local copies, waits for them, and re-layouts  1.3 us (3%)
    pallas_call x1, Pallas kernels, on_device(): pl.pallas_call(functools.partial(kernel, groups, devices), out_shape=jax....  37.6 us
    unnamed x1, local copies, waits for them, and re-layouts  1.3 us

profile of v7, /device:TPU:65, one launch (start us, length us, event | category | flops | bytes accessed | tf_op | source)
XLA Modules:
  0.0 38.9 jit_solution(4748609326466919471)
XLA Ops:
  0.0 37.6 %shard_map.64 = bf16[4,4,256]{2,1,0:T(4,128)(2,1)} custom-call(bf16[4,4,256]{2,1,0:T(4,128)(2,1)} %vol.1, bf16[9,3,32,32]{3,2,1,0:T(8,128)(2,1)} %bitcast.4, bf16[9,3,32,32]{3,2,1,0:T(8,128)(2,1)} %bitcast.5, bf16[256,512]{1,0:T(8,128)(2,1)} %wl.1, bf16[9,3,16,512]{3,2,1,0:T(8,128)(2,1)} %bitcast.3, bf16[512,512]{1,0:T(8,128)(2,1)} %wu.1), custom_call_target="tpu_custom_call" | custom-call | tf_op jit(solution)/shard_map/pallas_call | solution.py:473
  37.6 1.3 %copy.8 = bf16[4,4,256]{2,1,0:T(4,128)(2,1)} copy(bf16[4,4,256]{2,1,0:T(4,128)(2,1)} %shard_map.64) | data formatting | bytes 16384

commit v8 on v7

--- a/solution.py
+++ b/solution.py
@@ -11,7 +11,7 @@
 BF16 = jnp.bfloat16
 MESH = pl.DeviceIdType.MESH
 BANDS = [(zi, zo) for zo in range(4) for zi in range(4) if abs(zi - zo) <= 1]
-CHUNKS = [(0, 4), (4, 7), (7, 9)]
+CHUNKS = [(0, 3), (3, 5), (5, 7), (7, 8), (8, 9)]
 GAPS = [(zi, zo) for zo in range(4) for zi in range(4) if abs(zi - zo) > 1]
 
 
@@ -55,7 +55,7 @@
     groups, devices,
     vol, w1, w2, wl, wc, wu,
     out,
-    block_v, blocks, w1_v, w2_v, wl_v, wu_v, t1, t2, wq, raw, tc, wide, first, skip_p, send, recv, flat, cols, sums, parts, shares,
+    block_v, blocks, w1_v, w2_v, wl_v, wu_v, t1, t2, wq, raw, tc, wide, first, skip_p, send, recv, flat, cols, own_sums, sums, parts, shares,
     load_sem, twin_sem, halo_s, halo_r, raw_s, raw_r, fwd_s, fwd_r, side_s, side_r, a2a_s, a2a_r, rs_s, rs_r,
 ):
     g = lax.axis_index("grp")
@@ -141,6 +141,26 @@
     blocks[4] = block_v[...].astype(F32).reshape(16, 256).astype(BF16)
     pl.semaphore_wait(barrier, greeted + len(partners))
 
+    def cross(i, to_core):
+        lo, hi = CHUNKS[i]
+        return pltpu.make_async_remote_copy(
+            src_ref=wq.at[2 * to_core + xp, lo:hi],
+            dst_ref=raw.at[mine, xp, lo:hi],
+            send_sem=raw_s.at[2 * i + to_core],
+            recv_sem=raw_r.at[2 * i + core],
+            device_id=across(to_core),
+            device_id_type=MESH,
+        )
+
+    for c in quarters:
+        c.wait()
+
+    @pl.when(edge)
+    def _():
+        for i in range(len(CHUNKS)):
+            for to_core in range(2):
+                cross(i, to_core).start()
+
     def block_copy(dx, dy, slot):
         return pltpu.make_async_remote_copy(
             src_ref=blocks.at[4],
@@ -157,8 +177,6 @@
         def _():
             block_copy(dx, dy, (1 - dx) * 3 + 1 - dy).start()
 
-    for c in quarters:
-        c.wait()
     twin = pltpu.make_async_remote_copy(
         src_ref=wq.at[pl.ds(2 - 2 * core, 2)],
         dst_ref=raw.at[mine],
@@ -169,17 +187,6 @@
     )
     twin.start()
 
-    def cross(i, to_core):
-        lo, hi = CHUNKS[i]
-        return pltpu.make_async_remote_copy(
-            src_ref=wq.at[2 * to_core + xp, lo:hi],
-            dst_ref=raw.at[mine, xp, lo:hi],
-            send_sem=raw_s.at[2 * i + to_core],
-            recv_sem=raw_r.at[2 * i + core],
-            device_id=across(to_core),
-            device_id_type=MESH,
-        )
-
     foreign = 2 * (1 - zh)
 
     def onward(i, sideways):
@@ -193,12 +200,6 @@
             device_id=aside if sideways else (jnp.where(zl == 0, g + 1, g - 1), d),
             device_id_type=MESH,
         )
-
-    @pl.when(edge)
-    def _():
-        for i in range(len(CHUNKS)):
-            for to_core in range(2):
-                cross(i, to_core).start()
 
     def crossed(i, block):
         lo, hi = CHUNKS[i]
@@ -224,14 +225,13 @@
                     onward(i, False).wait_recv()
                 onward(i, True).start()
 
-    def banded(block, source):
-        for h in range(2):
-            for zi, zo in BANDS:
-                at = zo * width + h * part
-                tc[:, zi, block, :, at : at + part] = source[h][:, zi - zo + 1]
+    def banded(z_half, block, h, source):
+        for zi, zo in BANDS:
+            at = pl.multiple_of(zo * width + h * part, part)
+            tc[z_half, :, zi, block, :, pl.ds(at, part)] = source[:, zi - zo + 1]
 
     for zi, zo in GAPS:
-        tc[:, zi, :, :, zo * width : zo * width + width] = jnp.zeros((9, 4, 16, width), BF16)
+        tc[:, :, zi, :, :, zo * width : zo * width + width] = jnp.zeros((2, 9, 2, 16, width), BF16)
     wide[144:152] = jnp.zeros((8, 256), F32)
     first[120:128] = jnp.zeros((8, 256), F32)
     loads[0].wait()
@@ -240,7 +240,8 @@
     band_weights(w2_v, t2)
     for c in loads[2:]:
         c.wait()
-    banded(mine, [wq.at[2 * core + h] for h in range(2)])
+    for h in range(2):
+        banded(zh, core, h, wq.at[2 * core + h])
 
     row, col = iota((144, 144), 0), iota((144, 144), 1)
     slot = col >> 4
@@ -300,7 +301,12 @@
     lifted = gelu(dot(stacked.astype(BF16), wl_v[...]))
     for t in range(ring):
         send[t] = jnp.concatenate(
-            [lifted[k * 16 : k * 16 + 16, t * 64 : t * 64 + 64] for k in range(4)], axis=1
+            [
+                lifted[k * 16 : k * 16 + 16, t * 64 + h * 32 : t * 64 + h * 32 + 32]
+                for h in range(2)
+                for k in range(4)
+            ],
+            axis=1,
         ).astype(BF16)
 
     me = 2 * ry + core
@@ -321,7 +327,8 @@
         spread(m).start()
     recv[me] = send[ry]
     twin.wait_recv()
-    banded(2 * zh + 1 - core, [raw.at[2 * zh + 1 - core, h] for h in range(2)])
+    for h in range(2):
+        banded(zh, 1 - core, h, raw.at[2 * zh + 1 - core, h])
     pass_on(True)
     pass_on(False)
 
@@ -349,8 +356,19 @@
                     for b in range(3):
                         ox, oy = xx - a, yb - b
                         if 0 <= ox < 2 and 0 <= oy < 2:
-                            at, to = (2 * ox + oy) * half, (3 * a + b) * 256 + lt * 128
-                            cols[at : at + half, to : to + 128] = piece
+                            at, to = (2 * ox + oy) * half, (3 * a + b) * 128
+                            cols[lt, at : at + half, to : to + 128] = piece
+
+    def product(z_half, z):
+        return dot(
+            cols[z_half],
+            tc[z_half, :, :, :, :, z * width : z * width + width].reshape(1152, width),
+        )
+
+    for z in range(4):
+        own_sums[z] = product(zh, z)
+    for block in range(2):
+        banded(1 - zh, block, xp, raw.at[foreign + block, xp])
 
     for i in range(len(CHUNKS)):
         lo, hi = CHUNKS[i]
@@ -364,11 +382,10 @@
             device_id_type=MESH,
         ).wait_recv()
     for block in range(2):
-        banded(foreign + block, [raw.at[foreign + block, h] for h in range(2)])
-
-    lhs = cols[...]
+        banded(1 - zh, block, 1 - xp, raw.at[foreign + block, 1 - xp])
+
     for z in range(4):
-        got = dot(lhs, tc[:, :, :, :, z * width : z * width + width].reshape(2304, width))
+        got = own_sums[z] + product(1 - zh, z)
         for q in range(4):
             for lt in range(width // tile):
                 sums[lt, pl.ds(4 * z + q, half, stride=16), :] = got[
@@ -486,14 +503,15 @@
             pltpu.VMEM((9, 256, 256), BF16),
             pltpu.VMEM((4, 9, 3, 16, wide // 4), BF16),
             pltpu.VMEM((4, 2, 9, 3, 16, wide // 4), BF16),
-            pltpu.VMEM((9, 4, 4, 16, 2 * wide), BF16),
+            pltpu.VMEM((2, 9, 4, 2, 16, 2 * wide), BF16),
             pltpu.VMEM((152, 256), F32),
             pltpu.VMEM((128, 256), F32),
             pltpu.VMEM((64, 256), F32),
             pltpu.VMEM((devices // 4, 16, 256), BF16),
             pltpu.VMEM((half, 16, 256), BF16),
             pltpu.VMEM((2, 16 * half, 128), F32),
-            pltpu.VMEM((4 * half, 2304), BF16),
+            pltpu.VMEM((2, 4 * half, 1152), BF16),
+            pltpu.VMEM((4, 4 * half, wide // 2), F32),
             pltpu.VMEM((wide // 2 // tile, 16 * half, tile), F32),
             pltpu.VMEM((half, 16, wide // 2), BF16),
             pltpu.VMEM((half, 16, wide // 2), BF16),

time: 39.1 us -> 38.7 us (0.990)
  the two profiles are of different devices: /device:TPU:65 before, /device:TPU:7 now
where the time goes in v8:
time: 38.7 us; the launch traced here: 38.5 us
  Pallas kernels  37.2 us (96%)
  local copies, waits for them, and re-layouts  1.3 us (3%)
    pallas_call x1, Pallas kernels, on_device(): pl.pallas_call(functools.partial(kernel, groups, devices), out_shape=jax....  37.2 us
    unnamed x1, local copies, waits for them, and re-layouts  1.3 us

profile of v8, /device:TPU:7, one launch (start us, length us, event | category | flops | bytes accessed | tf_op | source)
XLA Modules:
  0.0 38.5 jit_solution(16740511951456803843)
XLA Ops:
  0.0 37.2 %shard_map.64 = bf16[4,4,256]{2,1,0:T(4,128)(2,1)} custom-call(bf16[4,4,256]{2,1,0:T(4,128)(2,1)} %vol.1, bf16[9,3,32,32]{3,2,1,0:T(8,128)(2,1)} %bitcast.4, bf16[9,3,32,32]{3,2,1,0:T(8,128)(2,1)} %bitcast.5, bf16[256,512]{1,0:T(8,128)(2,1)} %wl.1, bf16[9,3,16,512]{3,2,1,0:T(8,128)(2,1)} %bitcast.3, bf16[512,512]{1,0:T(8,128)(2,1)} %wu.1), custom_call_target="tpu_custom_call" | custom-call | tf_op jit(solution)/shard_map/pallas_call | solution.py:490
  37.2 1.3 %copy.8 = bf16[4,4,256]{2,1,0:T(4,128)(2,1)} copy(bf16[4,4,256]{2,1,0:T(4,128)(2,1)} %shard_map.64) | data formatting | bytes 16384

commit v9 on v8

--- a/solution.py
+++ b/solution.py
@@ -11,7 +11,7 @@
 BF16 = jnp.bfloat16
 MESH = pl.DeviceIdType.MESH
 BANDS = [(zi, zo) for zo in range(4) for zi in range(4) if abs(zi - zo) <= 1]
-CHUNKS = [(0, 3), (3, 5), (5, 7), (7, 8), (8, 9)]
+CHUNKS = [(0, 4), (4, 7), (7, 9)]
 GAPS = [(zi, zo) for zo in range(4) for zi in range(4) if abs(zi - zo) > 1]
 
 
@@ -152,15 +152,6 @@
             device_id_type=MESH,
         )
 
-    for c in quarters:
-        c.wait()
-
-    @pl.when(edge)
-    def _():
-        for i in range(len(CHUNKS)):
-            for to_core in range(2):
-                cross(i, to_core).start()
-
     def block_copy(dx, dy, slot):
         return pltpu.make_async_remote_copy(
             src_ref=blocks.at[4],
@@ -176,6 +167,15 @@
         @pl.when(exists(dx, dy))
         def _():
             block_copy(dx, dy, (1 - dx) * 3 + 1 - dy).start()
+
+    for c in quarters:
+        c.wait()
+
+    @pl.when(edge)
+    def _():
+        for i in range(len(CHUNKS)):
+            for to_core in range(2):
+                cross(i, to_core).start()
 
     twin = pltpu.make_async_remote_copy(
         src_ref=wq.at[pl.ds(2 - 2 * core, 2)],

time: 38.7 us -> 38.7 us (level)
  the two profiles are of different devices: /device:TPU:7 before, /device:TPU:65 now
where the time goes in v9:
time: 38.7 us; the launch traced here: 38.4 us
  Pallas kernels  37.1 us (96%)
  local copies, waits for them, and re-layouts  1.3 us (3%)
    pallas_call x1, Pallas kernels, on_device(): pl.pallas_call(functools.partial(kernel, groups, devices), out_shape=jax....  37.1 us
    unnamed x1, local copies, waits for them, and re-layouts  1.3 us

profile of v9, /device:TPU:65, one launch (start us, length us, event | category | flops | bytes accessed | tf_op | source)
XLA Modules:
  0.0 38.4 jit_solution(13443522209259455922)
XLA Ops:
  0.0 37.1 %shard_map.64 = bf16[4,4,256]{2,1,0:T(4,128)(2,1)} custom-call(bf16[4,4,256]{2,1,0:T(4,128)(2,1)} %vol.1, bf16[9,3,32,32]{3,2,1,0:T(8,128)(2,1)} %bitcast.4, bf16[9,3,32,32]{3,2,1,0:T(8,128)(2,1)} %bitcast.5, bf16[256,512]{1,0:T(8,128)(2,1)} %wl.1, bf16[9,3,16,512]{3,2,1,0:T(8,128)(2,1)} %bitcast.3, bf16[512,512]{1,0:T(8,128)(2,1)} %wu.1), custom_call_target="tpu_custom_call" | custom-call | tf_op jit(solution)/shard_map/pallas_call | solution.py:490
  37.1 1.3 %copy.8 = bf16[4,4,256]{2,1,0:T(4,128)(2,1)} copy(bf16[4,4,256]{2,1,0:T(4,128)(2,1)} %shard_map.64) | data formatting | bytes 16384

commit v10 on v9

--- a/solution.py
+++ b/solution.py
@@ -11,7 +11,7 @@
 BF16 = jnp.bfloat16
 MESH = pl.DeviceIdType.MESH
 BANDS = [(zi, zo) for zo in range(4) for zi in range(4) if abs(zi - zo) <= 1]
-CHUNKS = [(0, 4), (4, 7), (7, 9)]
+CHUNKS = [(0, 3), (3, 5), (5, 7), (7, 8), (8, 9)]
 GAPS = [(zi, zo) for zo in range(4) for zi in range(4) if abs(zi - zo) > 1]
 
 

time: 38.7 us -> 38.2 us (0.987)
  the two profiles are of different devices: /device:TPU:65 before, /device:TPU:69 now
where the time goes in v10:
time: 38.2 us; the launch traced here: 37.9 us
  Pallas kernels  36.6 us (96%)
  local copies, waits for them, and re-layouts  1.3 us (3%)
    pallas_call x1, Pallas kernels, on_device(): pl.pallas_call(functools.partial(kernel, groups, devices), out_shape=jax....  36.6 us
    unnamed x1, local copies, waits for them, and re-layouts  1.3 us

profile of v10, /device:TPU:69, one launch (start us, length us, event | category | flops | bytes accessed | tf_op | source)
XLA Modules:
  0.0 37.9 jit_solution(18369465097753364282)
XLA Ops:
  0.0 36.6 %shard_map.64 = bf16[4,4,256]{2,1,0:T(4,128)(2,1)} custom-call(bf16[4,4,256]{2,1,0:T(4,128)(2,1)} %vol.1, bf16[9,3,32,32]{3,2,1,0:T(8,128)(2,1)} %bitcast.4, bf16[9,3,32,32]{3,2,1,0:T(8,128)(2,1)} %bitcast.5, bf16[256,512]{1,0:T(8,128)(2,1)} %wl.1, bf16[9,3,16,512]{3,2,1,0:T(8,128)(2,1)} %bitcast.3, bf16[512,512]{1,0:T(8,128)(2,1)} %wu.1), custom_call_target="tpu_custom_call" | custom-call | tf_op jit(solution)/shard_map/pallas_call | solution.py:490
  36.6 1.3 %copy.8 = bf16[4,4,256]{2,1,0:T(4,128)(2,1)} copy(bf16[4,4,256]{2,1,0:T(4,128)(2,1)} %shard_map.64) | data formatting | bytes 16384

commit v11 on v10

--- a/solution.py
+++ b/solution.py
@@ -326,11 +326,11 @@
     for m in members:
         spread(m).start()
     recv[me] = send[ry]
+    pass_on(True)
+    pass_on(False)
     twin.wait_recv()
     for h in range(2):
         banded(zh, 1 - core, h, raw.at[2 * zh + 1 - core, h])
-    pass_on(True)
-    pass_on(False)
 
     def arrive(off, carry):
         frm = lax.rem(me + off, half)

time: 38.2 us -> 38.1 us (level)
  no operation moved by 1% of the time
where the time goes in v11:
time: 38.1 us; the launch traced here: 37.8 us
  Pallas kernels  36.5 us (96%)
  local copies, waits for them, and re-layouts  1.3 us (3%)
    pallas_call x1, Pallas kernels, on_device(): pl.pallas_call(functools.partial(kernel, groups, devices), out_shape=jax....  36.5 us
    unnamed x1, local copies, waits for them, and re-layouts  1.3 us

profile of v11, /device:TPU:69, one launch (start us, length us, event | category | flops | bytes accessed | tf_op | source)
XLA Modules:
  0.0 37.8 jit_solution(9368512661046773315)
XLA Ops:
  0.0 36.5 %shard_map.64 = bf16[4,4,256]{2,1,0:T(4,128)(2,1)} custom-call(bf16[4,4,256]{2,1,0:T(4,128)(2,1)} %vol.1, bf16[9,3,32,32]{3,2,1,0:T(8,128)(2,1)} %bitcast.4, bf16[9,3,32,32]{3,2,1,0:T(8,128)(2,1)} %bitcast.5, bf16[256,512]{1,0:T(8,128)(2,1)} %wl.1, bf16[9,3,16,512]{3,2,1,0:T(8,128)(2,1)} %bitcast.3, bf16[512,512]{1,0:T(8,128)(2,1)} %wu.1), custom_call_target="tpu_custom_call" | custom-call | tf_op jit(solution)/shard_map/pallas_call | solution.py:490
  36.5 1.3 %copy.8 = bf16[4,4,256]{2,1,0:T(4,128)(2,1)} copy(bf16[4,4,256]{2,1,0:T(4,128)(2,1)} %shard_map.64) | data formatting | bytes 16384
